TPU v7x, 256 devices: a whole 4x4x8 slice. The times are simulated.
256 devices in a mesh: seq: 64 (over z, y, core), sp: 4 (over x).
Axes of the slice: x: 4, y: 4, z: 8, core: 2. Of those that a mesh axis runs over, the one named last changes fastest.
Arguments:
- frames_in: bfloat16 [384, 32, 32, 384], P('seq', 'sp'), may hold values from -6 to 6
- gain: float32 [384], replicated, may hold values from 0.1 to 1.9
- conv_weight: bfloat16 [3, 3, 3, 384, 384], replicated, may hold values from -0.0625 to 0.0625
- conv_bias: float32 [384], replicated, may hold values from -3 to 3
- time_weight: bfloat16 [3, 384, 384], replicated, may hold values from -0.1875 to 0.1875
- time_bias: float32 [384], replicated, may hold values from -3 to 3
- clip_lengths: int32 [16], replicated, may hold values from 1 to 6, 64 in all
Outputs:
- latent: bfloat16 [192, 32, 32, 384], P('seq', 'sp')
Inputs may be any that keep to these rules, and one draw needn't show every extreme that they name: `clip_lengths`: the clips cover the 64 groups in order; the longest clip has exactly 6 groups.
All inputs are finite; a program needn't handle non-finite values.
Results may differ from a plain program's by a relative error of at most 0.005.
Values may be sent and summed in bfloat16 or wider, within the bound.
A program may use at most 128 MiB of HBM per device.

v0:
```python
import jax
import jax.numpy as jnp
from jax import lax
from jax.sharding import PartitionSpec as P


def with_halo(cells, sides, width):
    for axis, dim in sides:
        count = lax.axis_size(axis)
        ends = count - 1
        head = lax.slice_in_dim(cells, 0, width, axis=dim)
        tail = lax.slice_in_dim(cells, cells.shape[dim] - width, cells.shape[dim], axis=dim)
        cells = jnp.concatenate(
            [
                lax.ppermute(tail, axis, [(i, (i + 1) % count) for i in range(ends)]),
                cells,
                lax.ppermute(head, axis, [((i + 1) % count, i) for i in range(ends)]),
            ],
            axis=dim,
        )
    return cells


def from_behind(block, axis, distance):
    devices = range(lax.axis_size(axis))
    route = [(i - distance, i) for i in devices if i - distance in devices]
    return lax.ppermute(block, axis, route)


def normalize(values, gain):
    scale = lax.rsqrt(jnp.mean(values * values, axis=-1, keepdims=True) + 1e-06)
    return jax.nn.silu(values * scale * gain).astype(jnp.bfloat16)


def convolve(stack, conv_weight, count):
    rows = stack.shape[1] - 2
    cols = stack.shape[2] - 2
    width = stack.shape[3]
    total = jnp.zeros((count * rows * cols, width), jnp.float32)
    for tap_t in range(3):
        for tap_r in range(3):
            slab = stack[tap_t : tap_t + count, tap_r : tap_r + rows]
            joined = jnp.concatenate([slab[:, :, tap_c : tap_c + cols] for tap_c in range(3)], -1)
            kernel = conv_weight[tap_t, tap_r].reshape(3 * width, width)
            total = total + jnp.dot(
                joined.reshape(-1, 3 * width), kernel, preferred_element_type=jnp.float32
            )
    return total.reshape(count, rows, cols, width)


def per_device(frames_in, gain, conv_weight, conv_bias, time_weight, time_bias, clip_lengths):
    count = frames_in.shape[0]
    width = frames_in.shape[3]
    x_float = frames_in.astype(jnp.float32)
    act = normalize(x_float, gain)
    rimmed = with_halo(act, (("sp", 1),), 1)
    padded = jnp.pad(rimmed, ((0, 0), (0, 0), (1, 1), (0, 0)))
    position = lax.axis_index("seq")
    starts = jnp.cumsum(clip_lengths) - clip_lengths
    opening = jnp.any(starts == position)
    earlier = from_behind(padded[count - 2 :], "seq", 1)
    earlier = jnp.where(opening, jnp.zeros_like(earlier), earlier)
    stack = jnp.concatenate([earlier, padded], 0)
    resid = (x_float + convolve(stack, conv_weight, count) + conv_bias).astype(jnp.bfloat16)
    before = from_behind(resid[count - 1 :], "seq", 1)
    before = jnp.where(opening, jnp.zeros_like(before), before)
    extended = jnp.concatenate([before, resid], 0)
    pairs = extended[:count].reshape((count // 2, 2) + extended.shape[1:])
    following = extended[2::2]

    def project(values, weight):
        return jnp.dot(values.reshape(-1, width), weight, preferred_element_type=jnp.float32)

    latent = (
        project(pairs[:, 0], time_weight[0])
        + project(pairs[:, 1], time_weight[1])
        + project(following, time_weight[2])
        + time_bias
    )
    return latent.reshape(following.shape).astype(jnp.bfloat16)


def solution(mesh):
    return jax.shard_map(
        per_device,
        mesh=mesh,
        in_specs=(P("seq", "sp", None, None), P(), P(), P(), P(), P(), P()),
        out_specs=P("seq", "sp", None, None),
        check_vma=False,
    )
```

profile of v0, /device:TPU:128, one launch (start us, length us, event | category | flops | bytes accessed | tf_op | source)
XLA Modules:
  0.0 91.9 jit_solution(12572199295696402379)
XLA Ops:
  0.0 1.7 %fusion.8 = f32[6,8,32]{2,1,0:T(8,128)S(1)} fusion(bf16[6,8,32,384]{3,2,1,0:T(8,128)(2,1)} %param.7), kind=kLoop, calls=%fused_computation.62 | loop fusion | flops 1767936 | bytes 1185792 | tf_op jit(solution)/shard_map/reduce_sum | solution.py:31
  1.7 2.4 %fusion.15 = bf16[6,8,32,384]{3,2,1,0:T(8,128)(2,1)S(1)} fusion(bf16[6,8,32,384]{3,2,1,0:T(8,128)(2,1)} %param.7, f32[384]{0:T(512)} %param.8, f32[6,8,32]{2,1,0:T(8,128)S(1)} %add_rsqrt_fusion), kind=kLoop, calls=%fused_computation.69 | loop fusion | flops 4718592 | bytes 2366976 | tf_op jit(solution)/shard_map/convert_element_type | solution.py:32
  4.2 3.4 %collective-permute-start = (bf16[6,1,32,384]{3,2,1,0:T(8,128)(2,1)S(1)}, bf16[6,1,32,384]{3,2,1,0:T(8,128)(2,1)S(1)}, u32[]{:S(2)}, u32[]{:S(2)}) collective-permute-start(bf16[6,1,32,384]{3,2,1,0:T(8,128)(2,1)S(1)} %get-tuple-element.42), channel_id=1, source_target_pairs={{0,1},{1,2},{2,3},{4,5},{5,6},{6,7},{8,9},{9,10},{10,11},{12,13},{... | collective-permute-start | bytes 442376 | tf_op jit(solution)/shard_map/ppermute | solution.py:15
  7.6 1.3 %collective-permute-start.1 = (bf16[6,1,32,384]{3,2,1,0:T(8,128)(2,1)S(1)}, bf16[6,1,32,384]{3,2,1,0:T(8,128)(2,1)S(1)}, u32[]{:S(2)}, u32[]{:S(2)}) collective-permute-start(bf16[6,1,32,384]{3,2,1,0:T(8,128)(2,1)S(1)} %get-tuple-element.43), channel_id=1, source_target_pairs={{1,0},{2,1},{3,2},{5,4},{6,5},{7,6},{9,8},{10,9},{11,10},{13,12},{... | collective-permute-start | bytes 442376 | tf_op jit(solution)/shard_map/ppermute | solution.py:17
  8.9 1.8 %collective-permute-done = bf16[6,1,32,384]{3,2,1,0:T(8,128)(2,1)S(1)} collective-permute-done((bf16[6,1,32,384]{3,2,1,0:T(8,128)(2,1)S(1)}, bf16[6,1,32,384]{3,2,1,0:T(8,128)(2,1)S(1)}, u32[]{:S(2)}, u32[]{:S(2)}) %collective-permute-start) | collective-permute-done | bytes 147488 | tf_op jit(solution)/shard_map/ppermute | solution.py:15
  10.7 4.1 %collective-permute-done.1 = bf16[6,1,32,384]{3,2,1,0:T(8,128)(2,1)S(1)} collective-permute-done((bf16[6,1,32,384]{3,2,1,0:T(8,128)(2,1)S(1)}, bf16[6,1,32,384]{3,2,1,0:T(8,128)(2,1)S(1)}, u32[]{:S(2)}, u32[]{:S(2)}) %collective-permute-start.1) | collective-permute-done | bytes 147488 | tf_op jit(solution)/shard_map/ppermute | solution.py:17
  14.8 1.0 %fusion.22 = bf16[6,10,34,384]{3,2,1,0:T(8,128)(2,1)S(1)} fusion(bf16[6,1,32,384]{3,2,1,0:T(8,128)(2,1)S(1)} %collective-permute-done.1, bf16[6,8,32,384]{3,2,1,0:T(8,128)(2,1)S(1)} %fusion.15, bf16[6,1,32,384]{3,2,1,0:T(8,128)(2,1)S(1)} %collective-permute-done), kind=kLoop, calls=%fused_computation.76 | loop fusion | flops 9400320 | bytes 3041280 | tf_op jit(solution)/shard_map/concatenate | solution.py:13
  15.8 1.0 %slice.228 = bf16[2,10,34,384]{3,2,1,0:T(8,128)(2,1)} slice(bf16[6,10,34,384]{3,2,1,0:T(8,128)(2,1)S(1)} %fusion.22), slice={[4:6], [0:10], [0:34], [0:384]} | slice | bytes 1044480 | tf_op jit(solution)/shard_map/slice | solution.py:61
  16.7 2.2 %collective-permute-start.2 = (bf16[2,10,34,384]{3,2,1,0:T(8,128)(2,1)}, bf16[2,10,34,384]{3,2,1,0:T(8,128)(2,1)}, u32[]{:S(2)}, u32[]{:S(2)}) collective-permute-start(bf16[2,10,34,384]{3,2,1,0:T(8,128)(2,1)} %slice.228), channel_id=1, source_target_pairs={{0,4},{4,8},{8,12},{12,16},{16,20},{20,24},{24,28},{28,32},{32,36}... | collective-permute-start | bytes 1566728 | tf_op jit(solution)/shard_map/ppermute | solution.py:27
  18.9 0.0 copy-done.1
  19.0 3.8 %fusion.49 = (bf16[1,1,3,384,384]{4,3,2,1,0:T(8,128)(2,1)}, bf16[1,1,3,384,384]{4,3,2,1,0:T(8,128)(2,1)}, bf16[1,1,3,384,384]{4,3,2,1,0:T(8,128)(2,1)}, bf16[1,1...) fusion(bf16[3,3,3,384,384]{4,3,2,1,0:T(8,128)(2,1)S(1)} %copy-d, ...), kind=kLoop, calls=%fused_computation.110 | loop fusion | bytes 15925248 | tf_op jit(solution)/shard_map/slice | solution.py:44
  22.8 0.0 copy-done.15
  22.8 0.1 copy.9
  22.9 0.1 reduce
  23.0 0.6 compare_reduce_fusion
  23.7 0.9 fusion.50
  24.5 7.4 %collective-permute-done.2 = bf16[2,10,34,384]{3,2,1,0:T(8,128)(2,1)} collective-permute-done((bf16[2,10,34,384]{3,2,1,0:T(8,128)(2,1)}, bf16[2,10,34,384]{3,2,1,0:T(8,128)(2,1)}, u32[]{:S(2)}, u32[]{:S(2)}) %collective-permute-start.2) | collective-permute-done | bytes 522272 | tf_op jit(solution)/shard_map/ppermute | solution.py:27
  31.9 1.8 %broadcast_select_fusion = bf16[2,10,34,384]{3,2,1,0:T(8,128)(2,1)S(1)} fusion(bf16[2,10,34,384]{3,2,1,0:T(8,128)(2,1)} %collective-permute-done.2, pred[]{:T(512)} %compare_reduce_fusion), kind=kLoop, calls=%fused_computation.99 | loop fusion | flops 261120 | bytes 1044481 | tf_op jit(solution)/shard_map/jit(_where)/select_n | solution.py:62
  33.7 2.8 %fusion.41 = (bf16[6,8,32,384]{3,2,1,0:T(8,128)(2,1)S(1)}, bf16[6,8,32,384]{3,2,1,0:T(8,128)(2,1)S(1)}, bf16[6,8,32,384]{3,2,1,0:T(8,128)(2,1)S(1)}, bf16[6,8,32...) fusion(bf16[6,10,34,384]{3,2,1,0:T(8,128)(2,1)S(1)} %fusion.22,, ...), kind=kLoop, calls=%fused_computation.97 | loop fusion | flops 5308416 | bytes 15433728 | tf_op jit(solution)/shard_map/concatenate | solution.py:63
  36.6 2.5 %fusion.25 = (bf16[6,8,32,384]{3,2,1,0:T(8,128)(2,1)S(1)}, bf16[6,8,32,384]{3,2,1,0:T(8,128)(2,1)S(1)}, bf16[6,8,32,384]{3,2,1,0:T(8,128)(2,1)S(1)}, bf16[6,8,32...) fusion(bf16[6,10,34,384]{3,2,1,0:T(8,128)(2,1)S(1)} %fusion.22,, ...), kind=kLoop, calls=%fused_computation.81 | loop fusion | flops 4718592 | bytes 11526144 | tf_op jit(solution)/shard_map/concatenate | solution.py:63
  39.1 3.3 %pad_maximum_fusion.3 = (bf16[6,8,32,1152]{3,2,1,0:T(8,128)(2,1)}, bf16[6,8,32,1152]{3,2,1,0:T(8,128)(2,1)}) fusion(bf16[6,8,32,384]{3,2,1,0:T(8,128)(2,1)S(1)} %get-tuple-element.17, bf16[6,8,32,384]{3,2,1,0:T(8,128)(2,1)S(1)} %get-tuple-element.16, bf16[6,8,32,384]{3,2,1,0:T(8,128)(2,1)S(1)} %get-tuple-element.15, ...), kind=kLoop, calls=%fused_computation.28 | loop fusion | flops 21233664 | bytes 14155776 | tf_op jit(solution)/shard_map/concatenate | solution.py:43
  42.4 5.8 %fusion.53 = f32[1536,384]{1,0:T(8,128)} fusion(bf16[1536,1152]{1,0:T(8,128)(2,1)} %bitcast.60, bf16[1152,384]{1,0:T(8,128)(2,1)} %bitcast.77), kind=kOutput, calls=%fused_computation.114 | convolution fusion | flops 1358954496 | bytes 6782976 | tf_op jit(solution)/shard_map/dot_general | solution.py:45
  48.2 3.6 %fusion.2 = (bf16[6,8,32,1152]{3,2,1,0:T(8,128)(2,1)}, bf16[6,8,32,1152]{3,2,1,0:T(8,128)(2,1)S(1)}, bf16[6,8,32,1152]{3,2,1,0:T(8,128)(2,1)}) fusion(bf16[6,1,32,384]{3,2,1,0:T(8,128)(2,1)S(1)} %collective-permute-done.1, bf16[6,8,32,384]{3,2,1,0:T(8,128)(2,1)S(1)} %fusion.15, bf16[6,8,32,384]{3,2,1,0:T(8,128)(2,1)S(1)} %get-tuple-element.32, ...), kind=kLoop, calls=%fused_computation.22 | loop fusion | flops 38928384 | bytes 19169280 | tf_op jit(solution)/shard_map/concatenate | solution.py:43
  51.8 0.0 copy-done.12
  51.8 4.2 %fusion.54 = f32[1536,384]{1,0:T(8,128)S(1)} fusion(bf16[1536,1152]{1,0:T(8,128)(2,1)} %bitcast.63, bf16[1152,384]{1,0:T(8,128)(2,1)S(1)} %bitcast.76), kind=kOutput, calls=%fused_computation.115 | convolution fusion | flops 1358954496 | bytes 6782976 | tf_op jit(solution)/shard_map/dot_general | solution.py:45
  56.1 0.0 copy-done.11
  56.1 2.1 %fusion.55 = f32[1536,384]{1,0:T(8,128)S(1)} fusion(bf16[1536,1152]{1,0:T(8,128)(2,1)S(1)} %bitcast.62, bf16[1152,384]{1,0:T(8,128)(2,1)S(1)} %bitcast.75), kind=kOutput, calls=%fused_computation.116 | convolution fusion | flops 1358954496 | bytes 6782976 | tf_op jit(solution)/shard_map/dot_general | solution.py:45
  58.2 0.0 copy-start.2
  58.2 0.0 copy-start.10
  58.2 0.0 copy-start.16
  58.2 0.9 %fusion.5 = bf16[6,8,32,1152]{3,2,1,0:T(8,128)(2,1)S(1)} fusion(bf16[6,10,34,384]{3,2,1,0:T(8,128)(2,1)S(1)} %fusion.22, bf16[2,10,34,384]{3,2,1,0:T(8,128)(2,1)S(1)} %broadcast_select_fusion, bf16[6,8,32,384]{3,2,1,0:T(8,128)(2,1)S(1)} %get-tuple-element.23, bf16[6,8,32,384]{3,2,1,0:T(8,128)(2,1)S(1)} %get-tuple-element.14), kind=kLoop, calls=%fused_computation.27 | loop fusion | flops 14155776 | bytes 7987200 | tf_op jit(solution)/shard_map/concatenate | solution.py:43
  59.1 1.0 %copy-done.2 = bf16[6,8,32,1152]{3,2,1,0:T(8,128)(2,1)S(1)} copy-done((bf16[6,8,32,1152]{3,2,1,0:T(8,128)(2,1)S(1)}, bf16[6,8,32,1152]{3,2,1,0:T(8,128)(2,1)}, u32[]{:S(2)}) %copy-start.2) | copy-done | bytes 3538968
  60.2 0.2 copy-done.10
  60.4 0.8 copy-done.16
  61.2 2.2 %convolution_add_fusion.5 = f32[1536,384]{1,0:T(8,128)S(1)} fusion(f32[1536,384]{1,0:T(8,128)S(1)} %copy-done.16, bf16[1536,1152]{1,0:T(8,128)(2,1)S(1)} %bitcast.57, bf16[1152,384]{1,0:T(8,128)(2,1)S(1)} %bitcast.74), kind=kOutput, calls=%fused_computation.44 | convolution fusion | flops 1359544320 | bytes 9142272 | tf_op jit(solution)/shard_map/dot_general | solution.py:45
  63.4 0.0 copy-start.9
  63.4 1.0 %pad_maximum_fusion.5 = (bf16[6,8,32,1152]{3,2,1,0:T(8,128)(2,1)S(1)}, bf16[6,8,32,1152]{3,2,1,0:T(8,128)(2,1)S(1)}) fusion(bf16[6,8,32,384]{3,2,1,0:T(8,128)(2,1)S(1)} %get-tuple-element.24, bf16[6,8,32,384]{3,2,1,0:T(8,128)(2,1)S(1)} %get-tuple-element.22, bf16[6,8,32,384]{3,2,1,0:T(8,128)(2,1)S(1)} %get-tuple-element.21, ...), kind=kLoop, calls=%fused_computation.30 | loop fusion | flops 21233664 | bytes 14155776 | tf_op jit(solution)/shard_map/concatenate | solution.py:43
  64.4 0.1 copy-done.9
  64.6 2.1 %convolution_add_fusion.4 = f32[1536,384]{1,0:T(8,128)S(1)} fusion(f32[1536,384]{1,0:T(8,128)S(1)} %convolution_add_fusion.5, bf16[1536,1152]{1,0:T(8,128)(2,1)S(1)} %bitcast.59, bf16[1152,384]{1,0:T(8,128)(2,1)S(1)} %bitcast.73), kind=kOutput, calls=%fused_computation.43 | convolution fusion | flops 1359544320 | bytes 9142272 | tf_op jit(solution)/shard_map/dot_general | solution.py:45
  66.7 0.0 copy-done.8
  66.7 2.2 %convolution_add_fusion.3 = f32[1536,384]{1,0:T(8,128)S(1)} fusion(f32[1536,384]{1,0:T(8,128)S(1)} %convolution_add_fusion.4, bf16[1536,1152]{1,0:T(8,128)(2,1)S(1)} %bitcast.58, bf16[1152,384]{1,0:T(8,128)(2,1)S(1)} %bitcast.72), kind=kOutput, calls=%fused_computation.42 | convolution fusion | flops 1359544320 | bytes 9142272 | tf_op jit(solution)/shard_map/dot_general | solution.py:45
  68.9 0.0 copy-start.7
  68.9 0.4 pad_maximum_fusion.7
  69.3 0.7 copy-done.7
  70.1 2.2 %convolution_add_fusion.2 = f32[1536,384]{1,0:T(8,128)S(1)} fusion(f32[1536,384]{1,0:T(8,128)S(1)} %convolution_add_fusion.3, bf16[1536,1152]{1,0:T(8,128)(2,1)S(1)} %bitcast.64, bf16[1152,384]{1,0:T(8,128)(2,1)S(1)} %bitcast.71), kind=kOutput, calls=%fused_computation.41 | convolution fusion | flops 1359544320 | bytes 9142272 | tf_op jit(solution)/shard_map/dot_general | solution.py:45
  72.3 0.0 copy-done.4
  72.3 0.0 copy-start.3
  72.3 0.0 copy-start.6
  72.3 2.4 %fusion.7 = f32[1536,384]{1,0:T(8,128)S(1)} fusion(f32[1536,384]{1,0:T(8,128)S(1)} %fusion.55, f32[1536,384]{1,0:T(8,128)S(1)} %fusion.54, f32[1536,384]{1,0:T(8,128)S(1)} %convolution_add_fusion.2, bf16[1536,1152]{1,0:T(8,128)(2,1)S(1)} %bitcast.55, bf16[1152,384]{1,0:T(8,128)(2,1)S(1)} %bitcast.65), kind=kOutput, calls=%fused_computation.40 | convolution fusion | flops 1360723968 | bytes 13860864 | tf_op jit(solution)/shard_map/dot_general | solution.py:45
  74.7 0.0 copy-start
  74.7 0.0 copy-start.13
  74.7 2.1 %convolution_add_fusion = f32[1536,384]{1,0:T(8,128)S(1)} fusion(f32[1536,384]{1,0:T(8,128)S(1)} %fusion.7, bf16[1536,1152]{1,0:T(8,128)(2,1)S(1)} %bitcast.61, bf16[1152,384]{1,0:T(8,128)(2,1)S(1)} %bitcast.70), kind=kOutput, calls=%fused_computation.37 | convolution fusion | flops 1359544320 | bytes 9142272 | tf_op jit(solution)/shard_map/dot_general | solution.py:45
  76.8 0.5 fusion.17
  77.3 1.9 %collective-permute-start.3 = (bf16[1,8,32,384]{3,2,1,0:T(8,128)(2,1)S(1)}, bf16[1,8,32,384]{3,2,1,0:T(8,128)(2,1)S(1)}, u32[]{:S(2)}, u32[]{:S(2)}) collective-permute-start(bf16[1,8,32,384]{3,2,1,0:T(8,128)(2,1)S(1)} %slice.269), channel_id=1, source_target_pairs={{0,4},{4,8},{8,12},{12,16},{16,20},{20,24},{24,28},{28,32},{32,36}... | collective-permute-start | bytes 589832 | tf_op jit(solution)/shard_map/ppermute | solution.py:27
  79.3 0.1 slice.224
  79.3 8.3 %collective-permute-done.3 = bf16[1,8,32,384]{3,2,1,0:T(8,128)(2,1)S(1)} collective-permute-done((bf16[1,8,32,384]{3,2,1,0:T(8,128)(2,1)S(1)}, bf16[1,8,32,384]{3,2,1,0:T(8,128)(2,1)S(1)}, u32[]{:S(2)}, u32[]{:S(2)}) %collective-permute-start.3) | collective-permute-done | bytes 196640 | tf_op jit(solution)/shard_map/ppermute | solution.py:27
  87.6 0.7 broadcast_select_fusion.1
  88.3 0.0 copy-start.5
  88.3 0.1 pad_maximum_fusion.9
  88.5 0.1 fusion.51
  88.6 0.9 copy-done.5
  89.5 0.5 fusion.44
  90.0 0.5 convolution_add_fusion.7
  90.6 1.3 %fusion.24 = bf16[768,384]{1,0:T(8,128)(2,1)} fusion(f32[768,384]{1,0:T(8,128)S(1)} %convolution_add_fusion.7, bf16[768,384]{1,0:T(8,128)(2,1)S(1)} %bitcast.68, f32[384]{0:T(512)S(1)} %copy-done.14, bf16[3,384,384]{2,1,0:T(8,128)(2,1)S(1)} %copy-done.5), kind=kOutput, calls=%fused_computation.80 | convolution fusion | flops 227377152 | bytes 2656256 | tf_op jit(solution)/shard_map/dot_general | solution.py:72
  (16 shorter events, 0.1 us)
Async XLA Ops:
  0.0 18.9 %copy-start.1 = (bf16[3,3,3,384,384]{4,3,2,1,0:T(8,128)(2,1)S(1)}, bf16[3,3,3,384,384]{4,3,2,1,0:T(8,128)(2,1)}, u32[]{:S(2)}) copy-start(bf16[3,3,3,384,384]{4,3,2,1,0:T(8,128)(2,1)} %param.9) | copy-start | bytes 23887876
  4.2 6.5 %collective-permute-start = (bf16[6,1,32,384]{3,2,1,0:T(8,128)(2,1)S(1)}, bf16[6,1,32,384]{3,2,1,0:T(8,128)(2,1)S(1)}, u32[]{:S(2)}, u32[]{:S(2)}) collective-permute-start(bf16[6,1,32,384]{3,2,1,0:T(8,128)(2,1)S(1)} %get-tuple-element.42), channel_id=1, source_target_pairs={{0,1},{1,2},{2,3},{4,5},{5,6},{6,7},{8,9},{9,10},{10,11},{12,13},{... | collective-permute-start | bytes 442376 | tf_op jit(solution)/shard_map/ppermute | solution.py:15
  7.6 7.2 %collective-permute-start.1 = (bf16[6,1,32,384]{3,2,1,0:T(8,128)(2,1)S(1)}, bf16[6,1,32,384]{3,2,1,0:T(8,128)(2,1)S(1)}, u32[]{:S(2)}, u32[]{:S(2)}) collective-permute-start(bf16[6,1,32,384]{3,2,1,0:T(8,128)(2,1)S(1)} %get-tuple-element.43), channel_id=1, source_target_pairs={{1,0},{2,1},{3,2},{5,4},{6,5},{7,6},{9,8},{10,9},{11,10},{13,12},{... | collective-permute-start | bytes 442376 | tf_op jit(solution)/shard_map/ppermute | solution.py:17
  16.7 6.1 %copy-start.15 = (s32[16]{0:T(128)S(1)}, s32[16]{0:T(128)}, u32[]{:S(2)}) copy-start(s32[16]{0:T(128)} %param.13) | copy-start | bytes 196
  16.7 15.2 %collective-permute-start.2 = (bf16[2,10,34,384]{3,2,1,0:T(8,128)(2,1)}, bf16[2,10,34,384]{3,2,1,0:T(8,128)(2,1)}, u32[]{:S(2)}, u32[]{:S(2)}) collective-permute-start(bf16[2,10,34,384]{3,2,1,0:T(8,128)(2,1)} %slice.228), channel_id=1, source_target_pairs={{0,4},{4,8},{8,12},{12,16},{16,20},{20,24},{24,28},{28,32},{32,36}... | collective-permute-start | bytes 1566728 | tf_op jit(solution)/shard_map/ppermute | solution.py:27
  48.2 3.6 %copy-start.12 = (bf16[1,1,3,384,384]{4,3,2,1,0:T(8,128)(2,1)S(1)}, bf16[1,1,3,384,384]{4,3,2,1,0:T(8,128)(2,1)}, u32[]{:S(2)}) copy-start(bf16[1,1,3,384,384]{4,3,2,1,0:T(8,128)(2,1)} %get-tuple-element.6) | copy-start | bytes 2654212
  51.8 4.2 %copy-start.11 = (bf16[1,1,3,384,384]{4,3,2,1,0:T(8,128)(2,1)S(1)}, bf16[1,1,3,384,384]{4,3,2,1,0:T(8,128)(2,1)}, u32[]{:S(2)}) copy-start(bf16[1,1,3,384,384]{4,3,2,1,0:T(8,128)(2,1)} %get-tuple-element.13) | copy-start | bytes 2654212
  58.2 2.0 %copy-start.2 = (bf16[6,8,32,1152]{3,2,1,0:T(8,128)(2,1)S(1)}, bf16[6,8,32,1152]{3,2,1,0:T(8,128)(2,1)}, u32[]{:S(2)}) copy-start(bf16[6,8,32,1152]{3,2,1,0:T(8,128)(2,1)} %get-tuple-element.45) | copy-start | bytes 10616836
  58.2 2.2 %copy-start.10 = (bf16[1,1,3,384,384]{4,3,2,1,0:T(8,128)(2,1)S(1)}, bf16[1,1,3,384,384]{4,3,2,1,0:T(8,128)(2,1)}, u32[]{:S(2)}) copy-start(bf16[1,1,3,384,384]{4,3,2,1,0:T(8,128)(2,1)} %get-tuple-element.11) | copy-start | bytes 2654212
  58.2 3.0 %copy-start.16 = (f32[1536,384]{1,0:T(8,128)S(1)}, f32[1536,384]{1,0:T(8,128)}, u32[]{:S(2)}) copy-start(f32[1536,384]{1,0:T(8,128)} %fusion.53) | copy-start | bytes 7077892
  63.4 1.2 %copy-start.9 = (bf16[1,1,3,384,384]{4,3,2,1,0:T(8,128)(2,1)S(1)}, bf16[1,1,3,384,384]{4,3,2,1,0:T(8,128)(2,1)}, u32[]{:S(2)}) copy-start(bf16[1,1,3,384,384]{4,3,2,1,0:T(8,128)(2,1)} %get-tuple-element.10) | copy-start | bytes 2654212
  64.6 2.1 %copy-start.8 = (bf16[1,1,3,384,384]{4,3,2,1,0:T(8,128)(2,1)S(1)}, bf16[1,1,3,384,384]{4,3,2,1,0:T(8,128)(2,1)}, u32[]{:S(2)}) copy-start(bf16[1,1,3,384,384]{4,3,2,1,0:T(8,128)(2,1)} %get-tuple-element.9) | copy-start | bytes 2654212
  68.9 1.2 %copy-start.7 = (bf16[1,1,3,384,384]{4,3,2,1,0:T(8,128)(2,1)S(1)}, bf16[1,1,3,384,384]{4,3,2,1,0:T(8,128)(2,1)}, u32[]{:S(2)}) copy-start(bf16[1,1,3,384,384]{4,3,2,1,0:T(8,128)(2,1)} %get-tuple-element.8) | copy-start | bytes 2654212
  70.1 2.2 %copy-start.4 = (bf16[1,1,3,384,384]{4,3,2,1,0:T(8,128)(2,1)S(1)}, bf16[1,1,3,384,384]{4,3,2,1,0:T(8,128)(2,1)}, u32[]{:S(2)}) copy-start(bf16[1,1,3,384,384]{4,3,2,1,0:T(8,128)(2,1)} %get-tuple-element.7) | copy-start | bytes 2654212
  72.3 2.4 %copy-start.3 = (bf16[6,8,32,1152]{3,2,1,0:T(8,128)(2,1)S(1)}, bf16[6,8,32,1152]{3,2,1,0:T(8,128)(2,1)}, u32[]{:S(2)}) copy-start(bf16[6,8,32,1152]{3,2,1,0:T(8,128)(2,1)} %get-tuple-element.39) | copy-start | bytes 10616836
  72.3 2.4 %copy-start.6 = (bf16[1,1,3,384,384]{4,3,2,1,0:T(8,128)(2,1)S(1)}, bf16[1,1,3,384,384]{4,3,2,1,0:T(8,128)(2,1)}, u32[]{:S(2)}) copy-start(bf16[1,1,3,384,384]{4,3,2,1,0:T(8,128)(2,1)} %get-tuple-element.5) | copy-start | bytes 2654212
  74.7 2.1 %copy-start = (bf16[6,8,32,384]{3,2,1,0:T(8,128)(2,1)S(1)}, bf16[6,8,32,384]{3,2,1,0:T(8,128)(2,1)}, u32[]{:S(2)}) copy-start(bf16[6,8,32,384]{3,2,1,0:T(8,128)(2,1)} %param.7) | copy-start | bytes 3538948
  74.7 2.1 %copy-start.13 = (f32[384]{0:T(512)S(1)}, f32[384]{0:T(512)}, u32[]{:S(2)}) copy-start(f32[384]{0:T(512)} %param.10) | copy-start | bytes 4612
  77.3 10.3 %collective-permute-start.3 = (bf16[1,8,32,384]{3,2,1,0:T(8,128)(2,1)S(1)}, bf16[1,8,32,384]{3,2,1,0:T(8,128)(2,1)S(1)}, u32[]{:S(2)}, u32[]{:S(2)}) collective-permute-start(bf16[1,8,32,384]{3,2,1,0:T(8,128)(2,1)S(1)} %slice.269), channel_id=1, source_target_pairs={{0,4},{4,8},{8,12},{12,16},{16,20},{20,24},{24,28},{28,32},{32,36}... | collective-permute-start | bytes 589832 | tf_op jit(solution)/shard_map/ppermute | solution.py:27
  88.3 1.2 %copy-start.5 = (bf16[3,384,384]{2,1,0:T(8,128)(2,1)S(1)}, bf16[3,384,384]{2,1,0:T(8,128)(2,1)}, u32[]{:S(2)}) copy-start(bf16[3,384,384]{2,1,0:T(8,128)(2,1)} %param.11) | copy-start | bytes 2654212
  89.5 1.1 %copy-start.14 = (f32[384]{0:T(512)S(1)}, f32[384]{0:T(512)}, u32[]{:S(2)}) copy-start(f32[384]{0:T(512)} %param.12) | copy-start | bytes 4612
where the time goes:
time: 92.2 us; the launch traced here: 91.9 us
  matrix products  27.6 us (30%)
  other arithmetic  23.6 us (26%)
  waiting for transfers between devices  21.6 us (23%)
  local copies, waits for them, and re-layouts  9.82 us (11%)
  starting transfers between devices  8.84 us (10%)
    dot_general x9, matrix products, convolve(): jnp.dot(joined.reshape(-1, 3 * width), kernel, preferred_element_type=jnp...  25.3 us
    ppermute x2, waiting for transfers between devices, from_behind(): return lax.ppermute(block, axis, route)  15.7 us
    concatenate x5, other arithmetic, convolve(): jnp.concatenate([slab[:, :, tap_c:tap_c + cols] for tap_c in range(3)], -1)  9.27 us
    concatenate x2, other arithmetic, per_device(): stack = jnp.concatenate([earlier, padded], 0)  5.36 us
    ppermute x2, starting transfers between devices, from_behind(): return lax.ppermute(block, axis, route)  4.14 us
    ppermute x1, waiting for transfers between devices, with_halo(): lax.ppermute(head, axis, [((i + 1) % count, i) for i in range(ends)])  4.12 us
    unnamed x34, local copies, waits for them, and re-layouts  3.88 us
    slice x1, local copies, waits for them, and re-layouts, convolve(): kernel = conv_weight[tap_t, tap_r].reshape(3 * width, width)  3.82 us
  transfers between devices with their start and end apart: 4, of which 4 were waited for; matrix products, arithmetic and copies ran while one was open for 6% of the time, Pallas kernels for 0%

commit v1 on v0

v1 whole, which is shorter than its diff:
```python
import jax
import jax.numpy as jnp
from jax import lax
from jax.experimental import pallas as pl
from jax.experimental.pallas import tpu as pltpu
from jax.sharding import PartitionSpec as P

F32 = jnp.float32
BF16 = jnp.bfloat16
MESH = pl.DeviceIdType.MESH
TAPS = 3


def kernel(
    x_ref, gain_ref, cw_ref, cb_ref, tw_ref, tb_ref, clips_ref, out_ref,
    x_all, weight, time_w, vectors, joined, total, resid, before, latent,
    x_sem, w_sem, small_sem, send_sem, recv_sem, out_sem,
):
    frames, rows, cols, width = x_ref.shape
    lag = TAPS - 1
    seq_count, sp_count = lax.axis_size("seq"), lax.axis_size("sp")
    seq, sp = lax.axis_index("seq"), lax.axis_index("sp")
    seq_next, seq_back = lax.rem(seq + 1, seq_count), lax.rem(seq + seq_count - 1, seq_count)
    sp_next, sp_back = lax.rem(sp + 1, sp_count), lax.rem(sp + sp_count - 1, sp_count)

    loads = []
    for t in range(frames):
        loads.append(
            pltpu.make_async_copy(x_ref.at[t], x_all.at[lag + t, pl.ds(1, rows)], x_sem.at[t])
        )
    small = [
        pltpu.make_async_copy(source, vectors.at[pl.ds(8 * i, 1)], small_sem.at[i])
        for i, source in enumerate((gain_ref, cb_ref, tb_ref))
    ]
    weights = [
        pltpu.make_async_copy(
            cw_ref.at[k], weight.at[:, pl.ds(k * width, width)], w_sem.at[k]
        )
        for k in range(TAPS)
    ]
    time_load = pltpu.make_async_copy(tw_ref, time_w, w_sem.at[TAPS])
    small[0].start()
    for t in reversed(range(frames)):
        loads[t].start()
    for k in reversed(range(TAPS)):
        weights[k].start()
    time_load.start()
    small[1].start()
    small[2].start()

    barrier = pltpu.get_barrier_semaphore()
    for device in (
        (seq, sp_next), (seq, sp_back), (seq_back, sp), (seq_back, sp_next), (seq_back, sp_back)
    ):
        pl.semaphore_signal(barrier, inc=1, device_id=device, device_id_type=MESH)
    pl.semaphore_wait(barrier, 5)

    def send(slot, source, target, device):
        copy = pltpu.make_async_remote_copy(
            src_ref=source, dst_ref=target, send_sem=send_sem.at[slot], recv_sem=recv_sem.at[slot],
            device_id=device, device_id_type=MESH,
        )
        copy.start()
        return copy

    last = pl.ds(frames - lag, lag)
    own, past = pl.ds(lag, frames), pl.ds(0, lag)
    above = send(0, x_ref.at[:, rows - 1], x_all.at[own, 0], (seq, sp_next))
    below = send(1, x_ref.at[:, 0], x_all.at[own, rows + 1], (seq, sp_back))
    earlier = [
        send(2, x_ref.at[last], x_all.at[past, pl.ds(1, rows)], (seq_next, sp)),
        send(3, x_ref.at[last, rows - 1], x_all.at[past, 0], (seq_next, sp_next)),
        send(4, x_ref.at[last, 0], x_all.at[past, rows + 1], (seq_next, sp_back)),
    ]

    opening = jnp.int32(0)
    start = jnp.int32(0)
    for j in range(clips_ref.shape[0]):
        opening = opening + jnp.where(start == seq, 1, 0)
        start = start + clips_ref[j]
    keep = (1 - opening).astype(F32)
    has_above = jnp.where(sp > 0, 1, 0).astype(F32)
    has_below = jnp.where(sp < sp_count - 1, 1, 0).astype(F32)

    small[0].wait()
    half_gain = vectors[0:1] * 0.5
    column = lax.broadcasted_iota(jnp.int32, (cols, width), 0)

    def normalize(s, r, factor):
        values = x_all[s, r].astype(F32)
        scale = lax.rsqrt(jnp.mean(values * values, axis=-1, keepdims=True) + 1e-06)
        if factor is not None:
            scale = scale * factor
        half = values * scale * half_gain
        act = half + half * jnp.tanh(half)
        joined[s, r, :, pl.ds(width, width)] = act.astype(BF16)
        ahead = jnp.where(column == 0, 0.0, pltpu.roll(act, 1, 0))
        joined[s, r, :, pl.ds(0, width)] = ahead.astype(BF16)
        behind = jnp.where(column == cols - 1, 0.0, pltpu.roll(act, cols - 1, 0))
        joined[s, r, :, pl.ds(2 * width, width)] = behind.astype(BF16)

    def conv(s):
        left = jnp.concatenate(
            [joined[s, d : d + rows].reshape(rows * cols, TAPS * width) for d in range(TAPS)], 1
        )
        taps = [k for k in range(TAPS) if 0 <= s - k < frames]
        part = jnp.dot(
            left, weight[:, taps[0] * width : (taps[-1] + 1) * width], preferred_element_type=F32
        )
        for n, k in enumerate(taps):
            t = s - k
            piece = part[:, n * width : (n + 1) * width]
            if k == TAPS - 1 or s == frames + lag - 1:
                total[t] = piece
            elif k == 0:
                finish(t, total[t] + piece)
            else:
                total[t] = total[t] + piece

    def finish(t, summed):
        values = x_all[lag + t, 1 : rows + 1].reshape(rows * cols, width).astype(F32)
        resid[t + 1] = (values + summed + vectors[8:9]).astype(BF16)

    def project(j):
        left = jnp.concatenate([resid[2 * j + k] for k in range(TAPS)], 1)
        done = jnp.dot(left, time_w[...], preferred_element_type=F32) + vectors[16:17]
        latent[j] = done.reshape(rows, cols, width).astype(BF16)
        copy = pltpu.make_async_copy(latent.at[j], out_ref.at[j], out_sem.at[j])
        copy.start()
        return copy

    for t in reversed(range(frames)):
        loads[t].wait()
        for r in range(1, rows + 1):
            normalize(lag + t, r, None)
    above.wait_recv()
    below.wait_recv()
    for t in reversed(range(frames)):
        normalize(lag + t, 0, has_above)
        normalize(lag + t, rows + 1, has_below)
    small[1].wait()
    small[2].wait()
    weights[2].wait()
    conv(7)
    weights[1].wait()
    conv(6)
    weights[0].wait()
    conv(5)
    before_copy = send(5, resid.at[frames], before, (seq_next, sp))
    conv(4)
    conv(3)
    time_load.wait()
    outs = [project(2)]
    conv(2)
    for copy in earlier:
        copy.wait_recv()
    for s in reversed(range(lag)):
        normalize(s, 0, has_above * keep)
        for r in range(1, rows + 1):
            normalize(s, r, keep)
        normalize(s, rows + 1, has_below * keep)
    conv(1)
    outs.append(project(1))
    conv(0)
    before_copy.wait_recv()
    resid[0] = (before[...].astype(F32) * keep).astype(BF16)
    outs.append(project(0))
    for copy in [above, below, *earlier, before_copy]:
        copy.wait_send()
    for copy in outs:
        copy.wait()


def per_device(frames_in, gain, conv_weight, conv_bias, time_weight, time_bias, clip_lengths):
    frames, rows, cols, width = frames_in.shape
    deep = TAPS * TAPS * width
    lag = TAPS - 1
    anywhere = pl.BlockSpec(memory_space=pl.ANY)
    flops = 2 * frames * rows * cols * width * (TAPS * deep + TAPS * width // 2)
    return pl.pallas_call(
        kernel,
        out_shape=jax.ShapeDtypeStruct((frames // 2, rows, cols, width), BF16),
        in_specs=[anywhere] * 6 + [pl.BlockSpec(memory_space=pltpu.SMEM)],
        out_specs=anywhere,
        scratch_shapes=[
            pltpu.VMEM((frames + lag, rows + 2, cols, width), BF16),
            pltpu.VMEM((deep, TAPS * width), BF16),
            pltpu.VMEM((TAPS * width, width), BF16),
            pltpu.VMEM((24, width), F32),
            pltpu.VMEM((frames + lag, rows + 2, cols, TAPS * width), BF16),
            pltpu.VMEM((frames, rows * cols, width), F32),
            pltpu.VMEM((frames + 1, rows * cols, width), BF16),
            pltpu.VMEM((rows * cols, width), BF16),
            pltpu.VMEM((frames // 2, rows, cols, width), BF16),
            pltpu.SemaphoreType.DMA((frames,)),
            pltpu.SemaphoreType.DMA((TAPS + 1,)),
            pltpu.SemaphoreType.DMA((3,)),
            pltpu.SemaphoreType.DMA((6,)),
            pltpu.SemaphoreType.DMA((6,)),
            pltpu.SemaphoreType.DMA((frames // 2,)),
        ],
        compiler_params=pltpu.CompilerParams(
            collective_id=0, has_side_effects=True, vmem_limit_bytes=56 * 2**20
        ),
        cost_estimate=pl.CostEstimate(flops=flops, bytes_accessed=12_000_000, transcendentals=0),
        name="residual_block",
    )(
        frames_in,
        gain.reshape(1, width),
        conv_weight.reshape(TAPS, deep, width),
        conv_bias.reshape(1, width),
        time_weight.reshape(TAPS * width, width),
        time_bias.reshape(1, width),
        clip_lengths,
    )


def solution(mesh):
    return jax.shard_map(
        per_device,
        mesh=mesh,
        in_specs=(P("seq", "sp", None, None), P(), P(), P(), P(), P(), P()),
        out_specs=P("seq", "sp", None, None),
        check_vma=False,
    )
```

time: 92.2 us -> 34.6 us (0.38)
  the two profiles are of different devices: /device:TPU:128 before, /device:TPU:121 now
where the time goes in v1:
time: 34.6 us; the launch traced here: 34.4 us
  Pallas kernels  28.7 us (83%)
  local copies, waits for them, and re-layouts  5.72 us (17%)
    pallas_call x1, Pallas kernels, per_device(): pl.pallas_call(kernel, out_shape=jax.ShapeDtypeStruct((frames // 2, rows,...  28.7 us
    unnamed x1, local copies, waits for them, and re-layouts  1.94 us
    reshape x1, local copies, waits for them, and re-layouts, per_device(): conv_bias.reshape(1, width)  1.28 us
    reshape x1, local copies, waits for them, and re-layouts, per_device(): time_bias.reshape(1, width)  1.26 us
    reshape x1, local copies, waits for them, and re-layouts, per_device(): gain.reshape(1, width)  1.24 us

profile of v1, /device:TPU:121, one launch (start us, length us, event | category | flops | bytes accessed | tf_op | source)
XLA Modules:
  0.0 34.4 jit_solution(14479998401098629097)
XLA Ops:
  0.0 1.2 %reshape.15.gain_ref = f32[1,384]{1,0:T(1,128)} reshape(f32[384]{0:T(512)} %param.8) | data formatting | bytes 3072 | tf_op jit(solution)/shard_map/reshape | solution.py:209
  1.2 1.3 %reshape.17.cb_ref = f32[1,384]{1,0:T(1,128)} reshape(f32[384]{0:T(512)} %param.10) | data formatting | bytes 3072 | tf_op jit(solution)/shard_map/reshape | solution.py:211
  2.5 1.3 %reshape.19.tb_ref = f32[1,384]{1,0:T(1,128)} reshape(f32[384]{0:T(512)} %param.12) | data formatting | bytes 3072 | tf_op jit(solution)/shard_map/reshape | solution.py:213
  3.8 28.7 %residual_block.1 = bf16[3,8,32,384]{3,2,1,0:T(8,128)(2,1)} custom-call(bf16[6,8,32,384]{3,2,1,0:T(8,128)(2,1)} %x_ref.1, f32[1,384]{1,0:T(1,128)} %reshape.15.gain_ref, bf16[3,3456,384]{2,1,0:T(8,128)(2,1)} %bitcast.2, f32[1,384]{1,0:T(1,128)} %reshape.17.cb_ref, bf16[1152,384]{1,0:T(8,128)(2,1)} %bitcast.3, f32[1,384]{1,0:T(1,128)} %reshape.19.tb_ref, ...), custom_call_target="tpu_custom_call" | custom-call | flops 12910067712 | bytes 12000000 | tf_op jit(solution)/shard_map/residual_block/pallas_call | solution.py:180
  32.5 1.9 %copy.9 = bf16[3,8,32,384]{3,2,1,0:T(8,128)(2,1)} copy(bf16[3,8,32,384]{3,2,1,0:T(8,128)(2,1)} %residual_block.1) | data formatting | bytes 1179648

commit v2 on v1

v2 whole, which is shorter than its diff:
```python
import jax
import jax.numpy as jnp
from jax import lax
from jax.experimental import pallas as pl
from jax.experimental.pallas import tpu as pltpu
from jax.sharding import PartitionSpec as P

F32 = jnp.float32
BF16 = jnp.bfloat16
MESH = pl.DeviceIdType.MESH
TAPS = 3


def kernel(
    x_ref, gain_ref, cw_ref, cb_ref, tw_ref, tb_ref, clips_ref, out_ref,
    x_all, weight, time_w, gain_v, cb_v, tb_v, joined, total, resid, before, latent,
    x_sem, w_sem, small_sem, send_sem, recv_sem, out_sem,
):
    frames, rows, cols, width = x_ref.shape
    lag = TAPS - 1
    deep = TAPS * width
    seq_count, sp_count = lax.axis_size("seq"), lax.axis_size("sp")
    seq, sp = lax.axis_index("seq"), lax.axis_index("sp")
    seq_next, seq_back = lax.rem(seq + 1, seq_count), lax.rem(seq + seq_count - 1, seq_count)
    sp_next, sp_back = lax.rem(sp + 1, sp_count), lax.rem(sp + sp_count - 1, sp_count)

    barrier = pltpu.get_barrier_semaphore()
    for device in (
        (seq, sp_next), (seq, sp_back), (seq_back, sp), (seq_back, sp_next), (seq_back, sp_back)
    ):
        pl.semaphore_signal(barrier, inc=1, device_id=device, device_id_type=MESH)

    small = [
        pltpu.make_async_copy(source, target, small_sem.at[i])
        for i, (source, target) in enumerate(((gain_ref, gain_v), (cb_ref, cb_v), (tb_ref, tb_v)))
    ]
    loads = [
        pltpu.make_async_copy(x_ref.at[t], x_all.at[lag + t, pl.ds(1, rows)], x_sem.at[t])
        for t in range(frames)
    ]

    def weight_load(slot, first, size):
        return [
            pltpu.make_async_copy(
                cw_ref.at[k, pl.ds(first, size)],
                weight.at[pl.ds(first, size), pl.ds(k * width, width)],
                w_sem.at[slot + k],
            )
            for k in range(TAPS)
        ]

    head, tail = weight_load(0, 0, deep), weight_load(TAPS, deep, 2 * deep)
    time_load = pltpu.make_async_copy(tw_ref, time_w, w_sem.at[2 * TAPS])
    small[0].start()
    for t in (3, 2, 1, 5, 4, 0):
        loads[t].start()
    for copy in head:
        copy.start()

    pl.semaphore_wait(barrier, 5)

    def send(slot, source, target, device):
        copy = pltpu.make_async_remote_copy(
            src_ref=source, dst_ref=target, send_sem=send_sem.at[slot], recv_sem=recv_sem.at[slot],
            device_id=device, device_id_type=MESH,
        )
        copy.start()
        return copy

    last = pl.ds(frames - lag, lag)
    own, past = pl.ds(lag, frames), pl.ds(0, lag)
    above = send(0, x_ref.at[:, rows - 1], x_all.at[own, 0], (seq, sp_next))
    below = send(1, x_ref.at[:, 0], x_all.at[own, rows + 1], (seq, sp_back))
    earlier = [
        send(2, x_ref.at[last], x_all.at[past, pl.ds(1, rows)], (seq_next, sp)),
        send(3, x_ref.at[last, rows - 1], x_all.at[past, 0], (seq_next, sp_next)),
        send(4, x_ref.at[last, 0], x_all.at[past, rows + 1], (seq_next, sp_back)),
    ]

    opening = jnp.int32(0)
    start = jnp.int32(0)
    for j in range(clips_ref.shape[0]):
        opening = opening + jnp.where(start == seq, 1, 0)
        start = start + clips_ref[j]
    keep = (1 - opening).astype(F32)
    has_above = jnp.where(sp > 0, 1, 0).astype(F32)
    has_below = jnp.where(sp < sp_count - 1, 1, 0).astype(F32)

    small[0].wait()
    half_gain = gain_v[...].reshape(1, width) * 0.5
    column = lax.broadcasted_iota(jnp.int32, (cols, width), 0)

    def normalize(s, r, factor=None):
        values = x_all[s, r].astype(F32)
        scale = lax.rsqrt(jnp.mean(values * values, axis=-1, keepdims=True) + 1e-06)
        if factor is not None:
            scale = scale * factor
        half = values * scale * half_gain
        act = half + half * jnp.tanh(half)
        joined[s, r, :, pl.ds(width, width)] = act.astype(BF16)
        ahead = jnp.where(column == 0, 0.0, pltpu.roll(act, 1, 0))
        joined[s, r, :, pl.ds(0, width)] = ahead.astype(BF16)
        behind = jnp.where(column == cols - 1, 0.0, pltpu.roll(act, cols - 1, 0))
        joined[s, r, :, pl.ds(2 * width, width)] = behind.astype(BF16)

    queue = []

    def beside(count):
        for _ in range(min(count, len(queue))):
            normalize(*queue.pop(0))

    seen = set()
    inner, edge, whole = (1, rows - 1), None, (0, rows)

    def rows_of(s, part, d):
        if part is edge:
            pair = [joined[s, d], joined[s, rows - 1 + d]]
            return jnp.concatenate(pair, 0)
        lo, hi = part
        return joined[s, lo + d : hi + d].reshape((hi - lo) * cols, deep)

    def conv(sources, part, first=0, count=TAPS, final=()):
        left = jnp.concatenate(
            [
                jnp.concatenate([rows_of(s, part, d) for s in sources], 0)
                for d in range(first, first + count)
            ],
            1,
        )
        taps = [k for k in range(TAPS) if 0 <= sources[0] - k < frames]
        product = jnp.dot(
            left,
            weight[first * deep : (first + count) * deep, taps[0] * width : (taps[-1] + 1) * width],
            preferred_element_type=F32,
        )
        size = left.shape[0] // len(sources)
        sums = {}
        for i, s in enumerate(sources):
            for n, k in enumerate(taps):
                piece = product[i * size : (i + 1) * size, n * width : (n + 1) * width]
                sums[s - k] = sums[s - k] + piece if s - k in sums else piece
        for t, piece in sums.items():
            spots = [0, rows - 1] if part is edge else [slice(*part)]
            for i, spot in enumerate(spots):
                share = piece.shape[0] // len(spots)
                value = piece[i * share : (i + 1) * share]
                value = value.reshape(((share // cols,) if part is not edge else ()) + (cols, width))
                marks = [(t, r) for r in (range(*part) if part is not edge else [spot])]
                if marks[0] in seen:
                    value = total[t, spot] + value
                seen.update(marks)
                if t in final:
                    finish(t, value)
                else:
                    total[t, spot] = value

    def finish(t, summed):
        values = x_all[lag + t, 1 : rows + 1].astype(F32)
        done = values + summed + cb_v[...].reshape(1, 1, width)
        resid[t + 1] = done.reshape(rows * cols, width).astype(BF16)

    def project(j):
        left = jnp.concatenate([resid[2 * j + k] for k in range(TAPS)], 1)
        done = jnp.dot(left, time_w[...], preferred_element_type=F32) + tb_v[...].reshape(1, width)
        latent[j] = done.reshape(rows, cols, width).astype(BF16)
        copy = pltpu.make_async_copy(latent.at[j], out_ref.at[j], out_sem.at[j])
        copy.start()
        return copy

    for t in (3, 2, 1):
        loads[t].wait()
    for copy in tail + [time_load] + small[1:]:
        copy.start()
    for t in (3, 2, 1):
        for r in range(1, rows + 1):
            normalize(lag + t, r)
    for t in (5, 4, 0):
        loads[t].wait()
        queue.extend((lag + t, r) for r in range(1, rows + 1))
    for copy in head:
        copy.wait()
    for s in (5, 4, 3):
        conv((s,), inner, 0, 1)
        beside(4)
    for copy in tail + small[1:]:
        copy.wait()
    for s in (5, 4):
        conv((s,), inner, 1, 2)
        beside(6)
    above.wait_recv()
    below.wait_recv()
    for s in (5, 4, 3):
        normalize(s, 0, has_above)
        normalize(s, rows + 1, has_below)
    for s in (7, 6, 2):
        queue.append((s, 0, has_above))
        queue.append((s, rows + 1, has_below))
    conv((3,), inner, 1, 2)
    conv((5, 4, 3), edge)
    beside(len(queue))
    finish(3, total[3])
    conv((7,), whole)
    conv((6,), whole, final=(5, 4))
    before_copy = send(5, resid.at[frames], before, (seq_next, sp))
    time_load.wait()
    outs = [project(2)]
    for copy in earlier:
        copy.wait_recv()
    for s in reversed(range(lag)):
        normalize(s, 0, has_above * keep)
        for r in range(1, rows + 1):
            normalize(s, r, keep)
        normalize(s, rows + 1, has_below * keep)
    conv((2,), whole, final=(2,))
    conv((1,), whole, final=(1,))
    outs.append(project(1))
    conv((0,), whole, final=(0,))
    before_copy.wait_recv()
    resid[0] = (before[...].astype(F32) * keep).astype(BF16)
    outs.append(project(0))
    for copy in [above, below, *earlier, before_copy]:
        copy.wait_send()
    for copy in outs:
        copy.wait()


def per_device(frames_in, gain, conv_weight, conv_bias, time_weight, time_bias, clip_lengths):
    frames, rows, cols, width = frames_in.shape
    deep = TAPS * TAPS * width
    lag = TAPS - 1
    anywhere = pl.BlockSpec(memory_space=pl.ANY)
    flops = 2 * frames * rows * cols * width * (TAPS * deep + TAPS * width // 2)
    return pl.pallas_call(
        kernel,
        out_shape=jax.ShapeDtypeStruct((frames // 2, rows, cols, width), BF16),
        in_specs=[anywhere] * 6 + [pl.BlockSpec(memory_space=pltpu.SMEM)],
        out_specs=anywhere,
        scratch_shapes=[
            pltpu.VMEM((frames + lag, rows + 2, cols, width), BF16),
            pltpu.VMEM((deep, TAPS * width), BF16),
            pltpu.VMEM((TAPS * width, width), BF16),
            pltpu.VMEM((width,), F32),
            pltpu.VMEM((width,), F32),
            pltpu.VMEM((width,), F32),
            pltpu.VMEM((frames + lag, rows + 2, cols, TAPS * width), BF16),
            pltpu.VMEM((frames, rows, cols, width), F32),
            pltpu.VMEM((frames + 1, rows * cols, width), BF16),
            pltpu.VMEM((rows * cols, width), BF16),
            pltpu.VMEM((frames // 2, rows, cols, width), BF16),
            pltpu.SemaphoreType.DMA((frames,)),
            pltpu.SemaphoreType.DMA((2 * TAPS + 1,)),
            pltpu.SemaphoreType.DMA((3,)),
            pltpu.SemaphoreType.DMA((6,)),
            pltpu.SemaphoreType.DMA((6,)),
            pltpu.SemaphoreType.DMA((frames // 2,)),
        ],
        compiler_params=pltpu.CompilerParams(
            collective_id=0, has_side_effects=True, vmem_limit_bytes=56 * 2**20
        ),
        cost_estimate=pl.CostEstimate(flops=flops, bytes_accessed=12_000_000, transcendentals=0),
        name="residual_block",
    )(
        frames_in,
        gain,
        conv_weight.reshape(TAPS, deep, width),
        conv_bias,
        time_weight.reshape(TAPS * width, width),
        time_bias,
        clip_lengths,
    )


def solution(mesh):
    return jax.shard_map(
        per_device,
        mesh=mesh,
        in_specs=(P("seq", "sp", None, None), P(), P(), P(), P(), P(), P()),
        out_specs=P("seq", "sp", None, None),
        check_vma=False,
    )
```

time: 34.6 us -> 28.3 us (0.82)
  the two profiles are of different devices: /device:TPU:121 before, /device:TPU:2 now
where the time goes in v2:
time: 28.3 us; the launch traced here: 28.2 us
  Pallas kernels  26.3 us (93%)
  local copies, waits for them, and re-layouts  1.94 us (7%)
    pallas_call x1, Pallas kernels, per_device(): pl.pallas_call(kernel, out_shape=jax.ShapeDtypeStruct((frames // 2, rows,...  26.3 us
    unnamed x1, local copies, waits for them, and re-layouts  1.94 us

profile of v2, /device:TPU:2, one launch (start us, length us, event | category | flops | bytes accessed | tf_op | source)
XLA Modules:
  0.0 28.2 jit_solution(16788900359497576164)
XLA Ops:
  0.0 26.3 %residual_block.1 = bf16[3,8,32,384]{3,2,1,0:T(8,128)(2,1)} custom-call(bf16[6,8,32,384]{3,2,1,0:T(8,128)(2,1)} %x_ref.1, f32[384]{0:T(512)} %gain_ref.1, bf16[3,3456,384]{2,1,0:T(8,128)(2,1)} %bitcast.2, f32[384]{0:T(512)} %cb_ref.1, bf16[1152,384]{1,0:T(8,128)(2,1)} %bitcast.3, f32[384]{0:T(512)} %tb_ref.1, s32[16]{0:T(128)} %clips_ref.1), custom_call_target="tpu_custom_call" | custom-call | flops 12910067712 | bytes 12000000 | tf_op jit(solution)/shard_map/residual_block/pallas_call | solution.py:233
  26.3 1.9 %copy.9 = bf16[3,8,32,384]{3,2,1,0:T(8,128)(2,1)} copy(bf16[3,8,32,384]{3,2,1,0:T(8,128)(2,1)} %residual_block.1) | data formatting | bytes 1179648

commit v3 on v2

--- a/solution.py
+++ b/solution.py
@@ -13,7 +13,7 @@
 
 def kernel(
     x_ref, gain_ref, cw_ref, cb_ref, tw_ref, tb_ref, clips_ref, out_ref,
-    x_all, weight, time_w, gain_v, cb_v, tb_v, joined, total, resid, before, latent,
+    x_all, weight, time_w, gain_v, cb_v, tb_v, clips, joined, total, resid, before, latent,
     x_sem, w_sem, small_sem, send_sem, recv_sem, out_sem,
 ):
     frames, rows, cols, width = x_ref.shape
@@ -21,18 +21,27 @@
     deep = TAPS * width
     seq_count, sp_count = lax.axis_size("seq"), lax.axis_size("sp")
     seq, sp = lax.axis_index("seq"), lax.axis_index("sp")
-    seq_next, seq_back = lax.rem(seq + 1, seq_count), lax.rem(seq + seq_count - 1, seq_count)
-    sp_next, sp_back = lax.rem(sp + 1, sp_count), lax.rem(sp + sp_count - 1, sp_count)
+    has_back, has_next = seq > 0, seq < seq_count - 1
+    has_above, has_below = sp > 0, sp < sp_count - 1
 
     barrier = pltpu.get_barrier_semaphore()
-    for device in (
-        (seq, sp_next), (seq, sp_back), (seq_back, sp), (seq_back, sp_next), (seq_back, sp_back)
-    ):
-        pl.semaphore_signal(barrier, inc=1, device_id=device, device_id_type=MESH)
+
+    def greet(condition, device):
+        @pl.when(condition)
+        def _():
+            pl.semaphore_signal(barrier, inc=1, device_id=device, device_id_type=MESH)
+
+    greet(has_above, (seq, sp - 1))
+    greet(has_below, (seq, sp + 1))
+    greet(has_back, (seq - 1, sp))
+    greet(has_back & has_above, (seq - 1, sp - 1))
+    greet(has_back & has_below, (seq - 1, sp + 1))
 
     small = [
         pltpu.make_async_copy(source, target, small_sem.at[i])
-        for i, (source, target) in enumerate(((gain_ref, gain_v), (cb_ref, cb_v), (tb_ref, tb_v)))
+        for i, (source, target) in enumerate((
+                (gain_ref, gain_v), (cb_ref, cb_v), (tb_ref, tb_v), (clips_ref, clips)
+            ))
     ]
     loads = [
         pltpu.make_async_copy(x_ref.at[t], x_all.at[lag + t, pl.ds(1, rows)], x_sem.at[t])
@@ -57,34 +66,50 @@
     for copy in head:
         copy.start()
 
-    pl.semaphore_wait(barrier, 5)
-
-    def send(slot, source, target, device):
-        copy = pltpu.make_async_remote_copy(
-            src_ref=source, dst_ref=target, send_sem=send_sem.at[slot], recv_sem=recv_sem.at[slot],
-            device_id=device, device_id_type=MESH,
-        )
-        copy.start()
-        return copy
+    def count(condition):
+        return jnp.where(condition, 1, 0)
+
+    beside_me = count(has_above) + count(has_below)
+    pl.semaphore_wait(barrier, beside_me + count(has_next) * (1 + beside_me))
+
+    class Send:
+        def __init__(self, slot, source, target, device, leaves, comes):
+            self.copy = pltpu.make_async_remote_copy(
+                src_ref=source, dst_ref=target,
+                send_sem=send_sem.at[slot], recv_sem=recv_sem.at[slot],
+                device_id=device, device_id_type=MESH,
+            )
+            self.leaves, self.comes = leaves, comes
+            pl.when(leaves)(self.copy.start)
+
+            @pl.when(jnp.logical_not(comes))
+            def _():
+                target[...] = jnp.zeros(target.shape, target.dtype)
+
+        def wait_recv(self):
+            pl.when(self.comes)(self.copy.wait_recv)
+
+        def wait_send(self):
+            pl.when(self.leaves)(self.copy.wait_send)
 
     last = pl.ds(frames - lag, lag)
     own, past = pl.ds(lag, frames), pl.ds(0, lag)
-    above = send(0, x_ref.at[:, rows - 1], x_all.at[own, 0], (seq, sp_next))
-    below = send(1, x_ref.at[:, 0], x_all.at[own, rows + 1], (seq, sp_back))
+    up, down = (seq, sp - 1), (seq, sp + 1)
+    above = Send(0, x_ref.at[:, rows - 1], x_all.at[own, 0], down, has_below, has_above)
+    below = Send(1, x_ref.at[:, 0], x_all.at[own, rows + 1], up, has_above, has_below)
     earlier = [
-        send(2, x_ref.at[last], x_all.at[past, pl.ds(1, rows)], (seq_next, sp)),
-        send(3, x_ref.at[last, rows - 1], x_all.at[past, 0], (seq_next, sp_next)),
-        send(4, x_ref.at[last, 0], x_all.at[past, rows + 1], (seq_next, sp_back)),
+        Send(
+            2, x_ref.at[last], x_all.at[past, pl.ds(1, rows)], (seq + 1, sp), has_next, has_back
+        ),
+        Send(
+            3, x_ref.at[last, rows - 1], x_all.at[past, 0], (seq + 1, sp + 1),
+            has_next & has_below, has_back & has_above,
+        ),
+        Send(
+            4, x_ref.at[last, 0], x_all.at[past, rows + 1], (seq + 1, sp - 1),
+            has_next & has_above, has_back & has_below,
+        ),
     ]
-
-    opening = jnp.int32(0)
-    start = jnp.int32(0)
-    for j in range(clips_ref.shape[0]):
-        opening = opening + jnp.where(start == seq, 1, 0)
-        start = start + clips_ref[j]
-    keep = (1 - opening).astype(F32)
-    has_above = jnp.where(sp > 0, 1, 0).astype(F32)
-    has_below = jnp.where(sp < sp_count - 1, 1, 0).astype(F32)
 
     small[0].wait()
     half_gain = gain_v[...].reshape(1, width) * 0.5
@@ -190,27 +215,30 @@
     above.wait_recv()
     below.wait_recv()
     for s in (5, 4, 3):
-        normalize(s, 0, has_above)
-        normalize(s, rows + 1, has_below)
+        normalize(s, 0)
+        normalize(s, rows + 1)
     for s in (7, 6, 2):
-        queue.append((s, 0, has_above))
-        queue.append((s, rows + 1, has_below))
+        queue.extend(((s, 0), (s, rows + 1)))
     conv((3,), inner, 1, 2)
     conv((5, 4, 3), edge)
     beside(len(queue))
     finish(3, total[3])
     conv((7,), whole)
     conv((6,), whole, final=(5, 4))
-    before_copy = send(5, resid.at[frames], before, (seq_next, sp))
+    before_copy = Send(5, resid.at[frames], before, (seq + 1, sp), has_next, has_back)
     time_load.wait()
     outs = [project(2)]
     for copy in earlier:
         copy.wait_recv()
+    opening = jnp.int32(0)
+    start = jnp.int32(0)
+    for j in range(clips.shape[0]):
+        opening = opening + jnp.where(start == seq, 1, 0)
+        start = start + clips[j]
+    keep = (1 - opening).astype(F32)
     for s in reversed(range(lag)):
-        normalize(s, 0, has_above * keep)
-        for r in range(1, rows + 1):
+        for r in range(rows + 2):
             normalize(s, r, keep)
-        normalize(s, rows + 1, has_below * keep)
     conv((2,), whole, final=(2,))
     conv((1,), whole, final=(1,))
     outs.append(project(1))
@@ -233,7 +261,7 @@
     return pl.pallas_call(
         kernel,
         out_shape=jax.ShapeDtypeStruct((frames // 2, rows, cols, width), BF16),
-        in_specs=[anywhere] * 6 + [pl.BlockSpec(memory_space=pltpu.SMEM)],
+        in_specs=[anywhere] * 7,
         out_specs=anywhere,
         scratch_shapes=[
             pltpu.VMEM((frames + lag, rows + 2, cols, width), BF16),
@@ -242,6 +270,7 @@
             pltpu.VMEM((width,), F32),
             pltpu.VMEM((width,), F32),
             pltpu.VMEM((width,), F32),
+            pltpu.SMEM(clip_lengths.shape, jnp.int32),
             pltpu.VMEM((frames + lag, rows + 2, cols, TAPS * width), BF16),
             pltpu.VMEM((frames, rows, cols, width), F32),
             pltpu.VMEM((frames + 1, rows * cols, width), BF16),
@@ -249,7 +278,7 @@
             pltpu.VMEM((frames // 2, rows, cols, width), BF16),
             pltpu.SemaphoreType.DMA((frames,)),
             pltpu.SemaphoreType.DMA((2 * TAPS + 1,)),
-            pltpu.SemaphoreType.DMA((3,)),
+            pltpu.SemaphoreType.DMA((4,)),
             pltpu.SemaphoreType.DMA((6,)),
             pltpu.SemaphoreType.DMA((6,)),
             pltpu.SemaphoreType.DMA((frames // 2,)),

time: 28.3 us -> 25.5 us (0.901)
  the two profiles are of different devices: /device:TPU:2 before, /device:TPU:121 now
where the time goes in v3:
time: 25.5 us; the launch traced here: 25.3 us
  Pallas kernels  23.4 us (92%)
  local copies, waits for them, and re-layouts  1.94 us (8%)
    pallas_call x1, Pallas kernels, per_device(): pl.pallas_call(kernel, out_shape=jax.ShapeDtypeStruct((frames // 2, rows,...  23.4 us
    unnamed x1, local copies, waits for them, and re-layouts  1.94 us

profile of v3, /device:TPU:121, one launch (start us, length us, event | category | flops | bytes accessed | tf_op | source)
XLA Modules:
  0.0 25.3 jit_solution(1678368130717813873)
XLA Ops:
  0.0 23.4 %residual_block.1 = bf16[3,8,32,384]{3,2,1,0:T(8,128)(2,1)} custom-call(bf16[6,8,32,384]{3,2,1,0:T(8,128)(2,1)} %x_ref.1, f32[384]{0:T(512)} %gain_ref.1, bf16[3,3456,384]{2,1,0:T(8,128)(2,1)} %bitcast.2, f32[384]{0:T(512)} %cb_ref.1, bf16[1152,384]{1,0:T(8,128)(2,1)} %bitcast.3, f32[384]{0:T(512)} %tb_ref.1, s32[16]{0:T(128)} %clips_ref.1), custom_call_target="tpu_custom_call" | custom-call | flops 12910067712 | bytes 12000000 | tf_op jit(solution)/shard_map/residual_block/pallas_call | solution.py:261
  23.4 1.9 %copy.9 = bf16[3,8,32,384]{3,2,1,0:T(8,128)(2,1)} copy(bf16[3,8,32,384]{3,2,1,0:T(8,128)(2,1)} %residual_block.1) | data formatting | bytes 1179648

commit v4 on v3

--- a/solution.py
+++ b/solution.py
@@ -9,6 +9,7 @@
 BF16 = jnp.bfloat16
 MESH = pl.DeviceIdType.MESH
 TAPS = 3
+PIECE = 256
 
 
 def kernel(
@@ -66,51 +67,6 @@
     for copy in head:
         copy.start()
 
-    def count(condition):
-        return jnp.where(condition, 1, 0)
-
-    beside_me = count(has_above) + count(has_below)
-    pl.semaphore_wait(barrier, beside_me + count(has_next) * (1 + beside_me))
-
-    class Send:
-        def __init__(self, slot, source, target, device, leaves, comes):
-            self.copy = pltpu.make_async_remote_copy(
-                src_ref=source, dst_ref=target,
-                send_sem=send_sem.at[slot], recv_sem=recv_sem.at[slot],
-                device_id=device, device_id_type=MESH,
-            )
-            self.leaves, self.comes = leaves, comes
-            pl.when(leaves)(self.copy.start)
-
-            @pl.when(jnp.logical_not(comes))
-            def _():
-                target[...] = jnp.zeros(target.shape, target.dtype)
-
-        def wait_recv(self):
-            pl.when(self.comes)(self.copy.wait_recv)
-
-        def wait_send(self):
-            pl.when(self.leaves)(self.copy.wait_send)
-
-    last = pl.ds(frames - lag, lag)
-    own, past = pl.ds(lag, frames), pl.ds(0, lag)
-    up, down = (seq, sp - 1), (seq, sp + 1)
-    above = Send(0, x_ref.at[:, rows - 1], x_all.at[own, 0], down, has_below, has_above)
-    below = Send(1, x_ref.at[:, 0], x_all.at[own, rows + 1], up, has_above, has_below)
-    earlier = [
-        Send(
-            2, x_ref.at[last], x_all.at[past, pl.ds(1, rows)], (seq + 1, sp), has_next, has_back
-        ),
-        Send(
-            3, x_ref.at[last, rows - 1], x_all.at[past, 0], (seq + 1, sp + 1),
-            has_next & has_below, has_back & has_above,
-        ),
-        Send(
-            4, x_ref.at[last, 0], x_all.at[past, rows + 1], (seq + 1, sp - 1),
-            has_next & has_above, has_back & has_below,
-        ),
-    ]
-
     small[0].wait()
     half_gain = gain_v[...].reshape(1, width) * 0.5
     column = lax.broadcasted_iota(jnp.int32, (cols, width), 0)
@@ -144,7 +100,7 @@
         lo, hi = part
         return joined[s, lo + d : hi + d].reshape((hi - lo) * cols, deep)
 
-    def conv(sources, part, first=0, count=TAPS, final=()):
+    def conv(sources, part, first=0, count=TAPS, final=(), rate=0):
         left = jnp.concatenate(
             [
                 jnp.concatenate([rows_of(s, part, d) for s in sources], 0)
@@ -153,11 +109,13 @@
             1,
         )
         taps = [k for k in range(TAPS) if 0 <= sources[0] - k < frames]
-        product = jnp.dot(
-            left,
-            weight[first * deep : (first + count) * deep, taps[0] * width : (taps[-1] + 1) * width],
-            preferred_element_type=F32,
-        )
+        deepest, stop = slice(first * deep, (first + count) * deep), (taps[-1] + 1) * width
+        pieces = []
+        for column in range(taps[0] * width, stop, PIECE):
+            columns = slice(column, min(column + PIECE, stop))
+            pieces.append(jnp.dot(left, weight[deepest, columns], preferred_element_type=F32))
+            beside(rate)
+        product = jnp.concatenate(pieces, 1)
         size = left.shape[0] // len(sources)
         sums = {}
         for i, s in enumerate(sources):
@@ -199,30 +157,85 @@
     for t in (3, 2, 1):
         for r in range(1, rows + 1):
             normalize(lag + t, r)
+    def count(condition):
+        return jnp.where(condition, 1, 0)
+
+    beside_me = count(has_above) + count(has_below)
+    pl.semaphore_wait(barrier, beside_me + count(has_next) * (1 + beside_me))
+
+    class Send:
+        def __init__(self, slot, source, target, device, leaves, comes):
+            self.copy = pltpu.make_async_remote_copy(
+                src_ref=source, dst_ref=target,
+                send_sem=send_sem.at[slot], recv_sem=recv_sem.at[slot],
+                device_id=device, device_id_type=MESH,
+            )
+            self.leaves, self.comes = leaves, comes
+            pl.when(leaves)(self.copy.start)
+
+            @pl.when(jnp.logical_not(comes))
+            def _():
+                target[...] = jnp.zeros(target.shape, target.dtype)
+
+        def wait_recv(self):
+            pl.when(self.comes)(self.copy.wait_recv)
+
+        def wait_send(self):
+            pl.when(self.leaves)(self.copy.wait_send)
+
+    last = pl.ds(frames - lag, lag)
+    past = pl.ds(0, lag)
+    up, down = (seq, sp - 1), (seq, sp + 1)
+
+    def edges(slot, first, size):
+        here, there = pl.ds(first, size), pl.ds(lag + first, size)
+        return [
+            Send(
+                slot, x_ref.at[here, rows - 1], x_all.at[there, 0], down, has_below, has_above
+            ),
+            Send(
+                slot + 1, x_ref.at[here, 0], x_all.at[there, rows + 1], up, has_above, has_below
+            ),
+        ]
+
+    middle = edges(6, 1, 3)
+    outer = edges(0, 4, 2) + edges(8, 0, 1)
+    earlier = [
+        Send(
+            2, x_ref.at[last], x_all.at[past, pl.ds(1, rows)], (seq + 1, sp), has_next, has_back
+        ),
+        Send(
+            3, x_ref.at[last, rows - 1], x_all.at[past, 0], (seq + 1, sp + 1),
+            has_next & has_below, has_back & has_above,
+        ),
+        Send(
+            4, x_ref.at[last, 0], x_all.at[past, rows + 1], (seq + 1, sp - 1),
+            has_next & has_above, has_back & has_below,
+        ),
+    ]
+
     for t in (5, 4, 0):
         loads[t].wait()
         queue.extend((lag + t, r) for r in range(1, rows + 1))
     for copy in head:
         copy.wait()
     for s in (5, 4, 3):
-        conv((s,), inner, 0, 1)
-        beside(4)
+        conv((s,), inner, 0, 1, rate=1)
     for copy in tail + small[1:]:
         copy.wait()
     for s in (5, 4):
-        conv((s,), inner, 1, 2)
-        beside(6)
-    above.wait_recv()
-    below.wait_recv()
-    for s in (5, 4, 3):
-        normalize(s, 0)
-        normalize(s, rows + 1)
-    for s in (7, 6, 2):
-        queue.extend(((s, 0), (s, rows + 1)))
-    conv((3,), inner, 1, 2)
-    conv((5, 4, 3), edge)
-    beside(len(queue))
+        conv((s,), inner, 1, 2, rate=1)
+    for copy in middle:
+        copy.wait_recv()
+    queue[:0] = [(s, r) for s in (5, 4, 3) for r in (0, rows + 1)]
+    conv((3,), inner, 1, 2, rate=2)
+    for copy in outer:
+        copy.wait_recv()
+    queue[:0] = [(s, r) for s in (7, 6) for r in (0, rows + 1)]
+    queue.extend((2, r) for r in (0, rows + 1))
+    conv((5, 4, 3), edge, rate=2)
     finish(3, total[3])
+    beside(len([item for item in queue if item[0] > 2]))
     conv((7,), whole)
     conv((6,), whole, final=(5, 4))
     before_copy = Send(5, resid.at[frames], before, (seq + 1, sp), has_next, has_back)
@@ -236,17 +249,16 @@
         opening = opening + jnp.where(start == seq, 1, 0)
         start = start + clips[j]
     keep = (1 - opening).astype(F32)
-    for s in reversed(range(lag)):
-        for r in range(rows + 2):
-            normalize(s, r, keep)
-    conv((2,), whole, final=(2,))
+    beside(len(queue))
+    queue.extend((s, r, keep) for s in reversed(range(lag)) for r in range(rows + 2))
+    conv((2,), whole, final=(2,), rate=4)
     conv((1,), whole, final=(1,))
     outs.append(project(1))
     conv((0,), whole, final=(0,))
     before_copy.wait_recv()
     resid[0] = (before[...].astype(F32) * keep).astype(BF16)
     outs.append(project(0))
-    for copy in [above, below, *earlier, before_copy]:
+    for copy in [*middle, *outer, *earlier, before_copy]:
         copy.wait_send()
     for copy in outs:
         copy.wait()
@@ -279,8 +291,8 @@
             pltpu.SemaphoreType.DMA((frames,)),
             pltpu.SemaphoreType.DMA((2 * TAPS + 1,)),
             pltpu.SemaphoreType.DMA((4,)),
-            pltpu.SemaphoreType.DMA((6,)),
-            pltpu.SemaphoreType.DMA((6,)),
+            pltpu.SemaphoreType.DMA((10,)),
+            pltpu.SemaphoreType.DMA((10,)),
             pltpu.SemaphoreType.DMA((frames // 2,)),
         ],
         compiler_params=pltpu.CompilerParams(

time: 25.5 us -> 25.1 us (0.984)
  Pallas kernels: 23.4 us -> 23 us
    pallas_call x1, Pallas kernels: 23.4 us -> 23 us  [per_device(): pl.pallas_call(kernel, out_shape=jax.ShapeDtypeStruct((frames // 2, rows,...]
where the time goes in v4:
time: 25.1 us; the launch traced here: 25 us
  Pallas kernels  23 us (92%)
  local copies, waits for them, and re-layouts  1.94 us (8%)
    pallas_call x1, Pallas kernels, per_device(): pl.pallas_call(kernel, out_shape=jax.ShapeDtypeStruct((frames // 2, rows,...  23 us
    unnamed x1, local copies, waits for them, and re-layouts  1.94 us

profile of v4, /device:TPU:121, one launch (start us, length us, event | category | flops | bytes accessed | tf_op | source)
XLA Modules:
  0.0 25.0 jit_solution(16360286763818290353)
XLA Ops:
  0.0 23.0 %residual_block.1 = bf16[3,8,32,384]{3,2,1,0:T(8,128)(2,1)} custom-call(bf16[6,8,32,384]{3,2,1,0:T(8,128)(2,1)} %x_ref.1, f32[384]{0:T(512)} %gain_ref.1, bf16[3,3456,384]{2,1,0:T(8,128)(2,1)} %bitcast.2, f32[384]{0:T(512)} %cb_ref.1, bf16[1152,384]{1,0:T(8,128)(2,1)} %bitcast.3, f32[384]{0:T(512)} %tb_ref.1, s32[16]{0:T(128)} %clips_ref.1), custom_call_target="tpu_custom_call" | custom-call | flops 12910067712 | bytes 12000000 | tf_op jit(solution)/shard_map/residual_block/pallas_call | solution.py:273
  23.0 1.9 %copy.9 = bf16[3,8,32,384]{3,2,1,0:T(8,128)(2,1)} copy(bf16[3,8,32,384]{3,2,1,0:T(8,128)(2,1)} %residual_block.1) | data formatting | bytes 1179648

commit v5 on v4

--- a/solution.py
+++ b/solution.py
@@ -157,6 +157,14 @@
     for t in (3, 2, 1):
         for r in range(1, rows + 1):
             normalize(lag + t, r)
+    for t in (5, 4, 0):
+        loads[t].wait()
+        queue.extend((lag + t, r) for r in range(1, rows + 1))
+    for copy in head:
+        copy.wait()
+    for s in (5, 4, 3):
+        conv((s,), inner, 0, 1, rate=1)
+
     def count(condition):
         return jnp.where(condition, 1, 0)
 
@@ -214,23 +222,15 @@
         ),
     ]
 
-    for t in (5, 4, 0):
-        loads[t].wait()
-        queue.extend((lag + t, r) for r in range(1, rows + 1))
-    for copy in head:
+    for copy in tail + small[1:]:
         copy.wait()
     for s in (5, 4, 3):
-        conv((s,), inner, 0, 1, rate=1)
-    for copy in tail + small[1:]:
-        copy.wait()
-    for s in (5, 4):
         conv((s,), inner, 1, 2, rate=1)
-    for copy in middle:
+    for copy in middle + outer:
         copy.wait_recv()
-    queue[:0] = [(s, r) for s in (5, 4, 3) for r in (0, rows + 1)]
-    conv((3,), inner, 1, 2, rate=2)
-    for copy in outer:
-        copy.wait_recv()
+    for s in (5, 4, 3):
+        normalize(s, 0)
+        normalize(s, rows + 1)
     queue[:0] = [(s, r) for s in (7, 6) for r in (0, rows + 1)]
     queue.extend((2, r) for r in (0, rows + 1))
     conv((5, 4, 3), edge, rate=2)

time: 25.1 us -> 25.6 us (1.020)
  the two profiles are of different devices: /device:TPU:121 before, /device:TPU:2 now
where the time goes in v5:
time: 25.6 us; the launch traced here: 25.4 us
  Pallas kernels  23.5 us (92%)
  local copies, waits for them, and re-layouts  1.94 us (8%)
    pallas_call x1, Pallas kernels, per_device(): pl.pallas_call(kernel, out_shape=jax.ShapeDtypeStruct((frames // 2, rows,...  23.5 us
    unnamed x1, local copies, waits for them, and re-layouts  1.94 us

profile of v5, /device:TPU:2, one launch (start us, length us, event | category | flops | bytes accessed | tf_op | source)
XLA Modules:
  0.0 25.4 jit_solution(14439076509023007359)
XLA Ops:
  0.0 23.5 %residual_block.1 = bf16[3,8,32,384]{3,2,1,0:T(8,128)(2,1)} custom-call(bf16[6,8,32,384]{3,2,1,0:T(8,128)(2,1)} %x_ref.1, f32[384]{0:T(512)} %gain_ref.1, bf16[3,3456,384]{2,1,0:T(8,128)(2,1)} %bitcast.2, f32[384]{0:T(512)} %cb_ref.1, bf16[1152,384]{1,0:T(8,128)(2,1)} %bitcast.3, f32[384]{0:T(512)} %tb_ref.1, s32[16]{0:T(128)} %clips_ref.1), custom_call_target="tpu_custom_call" | custom-call | flops 12910067712 | bytes 12000000 | tf_op jit(solution)/shard_map/residual_block/pallas_call | solution.py:273
  23.5 1.9 %copy.9 = bf16[3,8,32,384]{3,2,1,0:T(8,128)(2,1)} copy(bf16[3,8,32,384]{3,2,1,0:T(8,128)(2,1)} %residual_block.1) | data formatting | bytes 1179648

commit v6 on v4

--- a/solution.py
+++ b/solution.py
@@ -15,7 +15,7 @@
 def kernel(
     x_ref, gain_ref, cw_ref, cb_ref, tw_ref, tb_ref, clips_ref, out_ref,
     x_all, weight, time_w, gain_v, cb_v, tb_v, clips, joined, total, resid, before, latent,
-    x_sem, w_sem, small_sem, send_sem, recv_sem, out_sem,
+    x_sem, w_sem, small_sem, send_sem, recv_sem, out_sem, ready_sem,
 ):
     frames, rows, cols, width = x_ref.shape
     lag = TAPS - 1
@@ -27,16 +27,16 @@
 
     barrier = pltpu.get_barrier_semaphore()
 
-    def greet(condition, device):
+    def greet(condition, device, semaphore=barrier):
         @pl.when(condition)
         def _():
-            pl.semaphore_signal(barrier, inc=1, device_id=device, device_id_type=MESH)
+            pl.semaphore_signal(semaphore, inc=1, device_id=device, device_id_type=MESH)
 
     greet(has_above, (seq, sp - 1))
     greet(has_below, (seq, sp + 1))
-    greet(has_back, (seq - 1, sp))
-    greet(has_back & has_above, (seq - 1, sp - 1))
-    greet(has_back & has_below, (seq - 1, sp + 1))
+    greet(has_next, (seq + 1, sp))
+    greet(has_next & has_above, (seq + 1, sp - 1))
+    greet(has_next & has_below, (seq + 1, sp + 1))
 
     small = [
         pltpu.make_async_copy(source, target, small_sem.at[i])
@@ -62,10 +62,11 @@
     head, tail = weight_load(0, 0, deep), weight_load(TAPS, deep, 2 * deep)
     time_load = pltpu.make_async_copy(tw_ref, time_w, w_sem.at[2 * TAPS])
     small[0].start()
-    for t in (3, 2, 1, 5, 4, 0):
+    for t in (3, 2, 1):
         loads[t].start()
-    for copy in head:
-        copy.start()
+    head[2].start()
+    for t in (5, 4, 0):
+        loads[t].start()
 
     small[0].wait()
     half_gain = gain_v[...].reshape(1, width) * 0.5
@@ -100,7 +101,7 @@
         lo, hi = part
         return joined[s, lo + d : hi + d].reshape((hi - lo) * cols, deep)
 
-    def conv(sources, part, first=0, count=TAPS, final=(), rate=0):
+    def conv(sources, part, first=0, count=TAPS, final=(), rate=0, only=range(TAPS), midway=lambda: None):
         left = jnp.concatenate(
             [
                 jnp.concatenate([rows_of(s, part, d) for s in sources], 0)
@@ -108,12 +109,14 @@
             ],
             1,
         )
-        taps = [k for k in range(TAPS) if 0 <= sources[0] - k < frames]
+        taps = [k for k in only if 0 <= sources[0] - k < frames]
         deepest, stop = slice(first * deep, (first + count) * deep), (taps[-1] + 1) * width
         pieces = []
         for column in range(taps[0] * width, stop, PIECE):
             columns = slice(column, min(column + PIECE, stop))
             pieces.append(jnp.dot(left, weight[deepest, columns], preferred_element_type=F32))
+            if column == taps[0] * width + 2 * PIECE:
+                midway()
             beside(rate)
         product = jnp.concatenate(pieces, 1)
         size = left.shape[0] // len(sources)
@@ -152,7 +155,7 @@
 
     for t in (3, 2, 1):
         loads[t].wait()
-    for copy in tail + [time_load] + small[1:]:
+    for copy in [head[1], head[0], *tail, time_load, *small[1:]]:
         copy.start()
     for t in (3, 2, 1):
         for r in range(1, rows + 1):
@@ -161,7 +164,10 @@
         return jnp.where(condition, 1, 0)
 
     beside_me = count(has_above) + count(has_below)
-    pl.semaphore_wait(barrier, beside_me + count(has_next) * (1 + beside_me))
+    pl.semaphore_wait(barrier, beside_me + count(has_back) * (1 + beside_me))
+    greet(has_back, (seq - 1, sp), ready_sem)
+    greet(has_back & has_above, (seq - 1, sp - 1), ready_sem)
+    greet(has_back & has_below, (seq - 1, sp + 1), ready_sem)
 
     class Send:
         def __init__(self, slot, source, target, device, leaves, comes):
@@ -200,6 +206,16 @@
 
     middle = edges(6, 1, 3)
     outer = edges(0, 4, 2) + edges(8, 0, 1)
+    for t in (5, 4, 0):
+        loads[t].wait()
+        queue.extend((lag + t, r) for r in range(1, rows + 1))
+    head[2].wait()
+    conv((5,), inner, 0, 1, rate=1, only=(2,))
+
+    @pl.when(has_next)
+    def _():
+        pl.semaphore_wait(ready_sem, 1 + beside_me)
+
     earlier = [
         Send(
             2, x_ref.at[last], x_all.at[past, pl.ds(1, rows)], (seq + 1, sp), has_next, has_back
@@ -213,14 +229,12 @@
             has_next & has_above, has_back & has_below,
         ),
     ]
-
-    for t in (5, 4, 0):
-        loads[t].wait()
-        queue.extend((lag + t, r) for r in range(1, rows + 1))
-    for copy in head:
-        copy.wait()
+    for s in (4, 3):
+        conv((s,), inner, 0, 1, rate=1, only=(2,))
+    head[1].wait()
+    head[0].wait()
     for s in (5, 4, 3):
-        conv((s,), inner, 0, 1, rate=1)
+        conv((s,), inner, 0, 1, rate=1, only=(0, 1))
     for copy in tail + small[1:]:
         copy.wait()
     for s in (5, 4):
@@ -241,8 +255,6 @@
     before_copy = Send(5, resid.at[frames], before, (seq + 1, sp), has_next, has_back)
     time_load.wait()
     outs = [project(2)]
-    for copy in earlier:
-        copy.wait_recv()
     opening = jnp.int32(0)
     start = jnp.int32(0)
     for j in range(clips.shape[0]):
@@ -250,8 +262,14 @@
         start = start + clips[j]
     keep = (1 - opening).astype(F32)
     beside(len(queue))
-    queue.extend((s, r, keep) for s in reversed(range(lag)) for r in range(rows + 2))
-    conv((2,), whole, final=(2,), rate=4)
+
+    def take_past():
+        for copy in earlier:
+            copy.wait_recv()
+        queue.extend((s, r, keep) for s in reversed(range(lag)) for r in range(rows + 2))
+
+    conv((2,), whole, final=(2,), rate=6, midway=take_past)
+    beside(len(queue))
     conv((1,), whole, final=(1,))
     outs.append(project(1))
     conv((0,), whole, final=(0,))
@@ -294,6 +312,7 @@
             pltpu.SemaphoreType.DMA((10,)),
             pltpu.SemaphoreType.DMA((10,)),
             pltpu.SemaphoreType.DMA((frames // 2,)),
+            pltpu.SemaphoreType.REGULAR,
         ],
         compiler_params=pltpu.CompilerParams(
             collective_id=0, has_side_effects=True, vmem_limit_bytes=56 * 2**20

time: 25.1 us -> 28.6 us (1.14)
  Pallas kernels: 23 us -> 26.5 us
    pallas_call x1, Pallas kernels: 23 us -> 26.5 us  [per_device(): pl.pallas_call(kernel, out_shape=jax.ShapeDtypeStruct((frames // 2, rows,...]
where the time goes in v6:
time: 28.6 us; the launch traced here: 28.4 us
  Pallas kernels  26.5 us (93%)
  local copies, waits for them, and re-layouts  1.94 us (7%)
    pallas_call x1, Pallas kernels, per_device(): pl.pallas_call(kernel, out_shape=jax.ShapeDtypeStruct((frames // 2, rows,...  26.5 us
    unnamed x1, local copies, waits for them, and re-layouts  1.94 us

profile of v6, /device:TPU:121, one launch (start us, length us, event | category | flops | bytes accessed | tf_op | source)
XLA Modules:
  0.0 28.4 jit_solution(6278502628010479107)
XLA Ops:
  0.0 26.5 %residual_block.1 = bf16[3,8,32,384]{3,2,1,0:T(8,128)(2,1)} custom-call(bf16[6,8,32,384]{3,2,1,0:T(8,128)(2,1)} %x_ref.1, f32[384]{0:T(512)} %gain_ref.1, bf16[3,3456,384]{2,1,0:T(8,128)(2,1)} %bitcast.2, f32[384]{0:T(512)} %cb_ref.1, bf16[1152,384]{1,0:T(8,128)(2,1)} %bitcast.3, f32[384]{0:T(512)} %tb_ref.1, s32[16]{0:T(128)} %clips_ref.1), custom_call_target="tpu_custom_call" | custom-call | flops 12910067712 | bytes 12000000 | tf_op jit(solution)/shard_map/residual_block/pallas_call | solution.py:291
  26.5 1.9 %copy.9 = bf16[3,8,32,384]{3,2,1,0:T(8,128)(2,1)} copy(bf16[3,8,32,384]{3,2,1,0:T(8,128)(2,1)} %residual_block.1) | data formatting | bytes 1179648

commit v7 on v5

--- a/solution.py
+++ b/solution.py
@@ -15,7 +15,7 @@
 def kernel(
     x_ref, gain_ref, cw_ref, cb_ref, tw_ref, tb_ref, clips_ref, out_ref,
     x_all, weight, time_w, gain_v, cb_v, tb_v, clips, joined, total, resid, before, latent,
-    x_sem, w_sem, small_sem, send_sem, recv_sem, out_sem,
+    x_sem, w_sem, small_sem, send_sem, recv_sem, out_sem, ready_sem,
 ):
     frames, rows, cols, width = x_ref.shape
     lag = TAPS - 1
@@ -27,16 +27,16 @@
 
     barrier = pltpu.get_barrier_semaphore()
 
-    def greet(condition, device):
+    def greet(condition, device, semaphore=barrier):
         @pl.when(condition)
         def _():
-            pl.semaphore_signal(barrier, inc=1, device_id=device, device_id_type=MESH)
+            pl.semaphore_signal(semaphore, inc=1, device_id=device, device_id_type=MESH)
 
     greet(has_above, (seq, sp - 1))
     greet(has_below, (seq, sp + 1))
-    greet(has_back, (seq - 1, sp))
-    greet(has_back & has_above, (seq - 1, sp - 1))
-    greet(has_back & has_below, (seq - 1, sp + 1))
+    greet(has_next, (seq + 1, sp))
+    greet(has_next & has_above, (seq + 1, sp - 1))
+    greet(has_next & has_below, (seq + 1, sp + 1))
 
     small = [
         pltpu.make_async_copy(source, target, small_sem.at[i])
@@ -66,6 +66,53 @@
         loads[t].start()
     for copy in head:
         copy.start()
+
+    def count(condition):
+        return jnp.where(condition, 1, 0)
+
+    beside_me = count(has_above) + count(has_below)
+    pl.semaphore_wait(barrier, beside_me + count(has_back) * (1 + beside_me))
+    greet(has_back, (seq - 1, sp), ready_sem)
+    greet(has_back & has_above, (seq - 1, sp - 1), ready_sem)
+    greet(has_back & has_below, (seq - 1, sp + 1), ready_sem)
+
+    class Send:
+        def __init__(self, slot, source, target, device, leaves, comes):
+            self.copy = pltpu.make_async_remote_copy(
+                src_ref=source, dst_ref=target,
+                send_sem=send_sem.at[slot], recv_sem=recv_sem.at[slot],
+                device_id=device, device_id_type=MESH,
+            )
+            self.leaves, self.comes = leaves, comes
+            pl.when(leaves)(self.copy.start)
+
+            @pl.when(jnp.logical_not(comes))
+            def _():
+                target[...] = jnp.zeros(target.shape, target.dtype)
+
+        def wait_recv(self):
+            pl.when(self.comes)(self.copy.wait_recv)
+
+        def wait_send(self):
+            pl.when(self.leaves)(self.copy.wait_send)
+
+    last = pl.ds(frames - lag, lag)
+    past = pl.ds(0, lag)
+    up, down = (seq, sp - 1), (seq, sp + 1)
+
+    def edges(slot, first, size):
+        here, there = pl.ds(first, size), pl.ds(lag + first, size)
+        return [
+            Send(
+                slot, x_ref.at[here, rows - 1], x_all.at[there, 0], down, has_below, has_above
+            ),
+            Send(
+                slot + 1, x_ref.at[here, 0], x_all.at[there, rows + 1], up, has_above, has_below
+            ),
+        ]
+
+    middle = edges(6, 1, 3)
+    outer = edges(0, 4, 2) + edges(8, 0, 1)
 
     small[0].wait()
     half_gain = gain_v[...].reshape(1, width) * 0.5
@@ -100,7 +147,7 @@
         lo, hi = part
         return joined[s, lo + d : hi + d].reshape((hi - lo) * cols, deep)
 
-    def conv(sources, part, first=0, count=TAPS, final=(), rate=0):
+    def conv(sources, part, first=0, count=TAPS, final=(), rate=0, midway=lambda: None):
         left = jnp.concatenate(
             [
                 jnp.concatenate([rows_of(s, part, d) for s in sources], 0)
@@ -114,6 +161,8 @@
         for column in range(taps[0] * width, stop, PIECE):
             columns = slice(column, min(column + PIECE, stop))
             pieces.append(jnp.dot(left, weight[deepest, columns], preferred_element_type=F32))
+            if column == taps[0] * width + 2 * PIECE:
+                midway()
             beside(rate)
         product = jnp.concatenate(pieces, 1)
         size = left.shape[0] // len(sources)
@@ -165,49 +214,10 @@
     for s in (5, 4, 3):
         conv((s,), inner, 0, 1, rate=1)
 
-    def count(condition):
-        return jnp.where(condition, 1, 0)
-
-    beside_me = count(has_above) + count(has_below)
-    pl.semaphore_wait(barrier, beside_me + count(has_next) * (1 + beside_me))
-
-    class Send:
-        def __init__(self, slot, source, target, device, leaves, comes):
-            self.copy = pltpu.make_async_remote_copy(
-                src_ref=source, dst_ref=target,
-                send_sem=send_sem.at[slot], recv_sem=recv_sem.at[slot],
-                device_id=device, device_id_type=MESH,
-            )
-            self.leaves, self.comes = leaves, comes
-            pl.when(leaves)(self.copy.start)
-
-            @pl.when(jnp.logical_not(comes))
-            def _():
-                target[...] = jnp.zeros(target.shape, target.dtype)
-
-        def wait_recv(self):
-            pl.when(self.comes)(self.copy.wait_recv)
-
-        def wait_send(self):
-            pl.when(self.leaves)(self.copy.wait_send)
-
-    last = pl.ds(frames - lag, lag)
-    past = pl.ds(0, lag)
-    up, down = (seq, sp - 1), (seq, sp + 1)
-
-    def edges(slot, first, size):
-        here, there = pl.ds(first, size), pl.ds(lag + first, size)
-        return [
-            Send(
-                slot, x_ref.at[here, rows - 1], x_all.at[there, 0], down, has_below, has_above
-            ),
-            Send(
-                slot + 1, x_ref.at[here, 0], x_all.at[there, rows + 1], up, has_above, has_below
-            ),
-        ]
-
-    middle = edges(6, 1, 3)
-    outer = edges(0, 4, 2) + edges(8, 0, 1)
+    @pl.when(has_next)
+    def _():
+        pl.semaphore_wait(ready_sem, 1 + beside_me)
+
     earlier = [
         Send(
             2, x_ref.at[last], x_all.at[past, pl.ds(1, rows)], (seq + 1, sp), has_next, has_back
@@ -221,16 +231,16 @@
             has_next & has_above, has_back & has_below,
         ),
     ]
-
     for copy in tail + small[1:]:
         copy.wait()
-    for s in (5, 4, 3):
+    for s in (5, 4):
         conv((s,), inner, 1, 2, rate=1)
-    for copy in middle + outer:
+    for copy in middle:
         copy.wait_recv()
-    for s in (5, 4, 3):
-        normalize(s, 0)
-        normalize(s, rows + 1)
+    queue[:0] = [(s, r) for s in (5, 4, 3) for r in (0, rows + 1)]
+    conv((3,), inner, 1, 2, rate=2)
+    for copy in outer:
+        copy.wait_recv()
     queue[:0] = [(s, r) for s in (7, 6) for r in (0, rows + 1)]
     queue.extend((2, r) for r in (0, rows + 1))
     conv((5, 4, 3), edge, rate=2)
@@ -241,8 +251,6 @@
     before_copy = Send(5, resid.at[frames], before, (seq + 1, sp), has_next, has_back)
     time_load.wait()
     outs = [project(2)]
-    for copy in earlier:
-        copy.wait_recv()
     opening = jnp.int32(0)
     start = jnp.int32(0)
     for j in range(clips.shape[0]):
@@ -250,8 +258,14 @@
         start = start + clips[j]
     keep = (1 - opening).astype(F32)
     beside(len(queue))
-    queue.extend((s, r, keep) for s in reversed(range(lag)) for r in range(rows + 2))
-    conv((2,), whole, final=(2,), rate=4)
+
+    def take_past():
+        for copy in earlier:
+            copy.wait_recv()
+        queue.extend((s, r, keep) for s in reversed(range(lag)) for r in range(rows + 2))
+
+    conv((2,), whole, final=(2,), rate=6, midway=take_past)
+    beside(len(queue))
     conv((1,), whole, final=(1,))
     outs.append(project(1))
     conv((0,), whole, final=(0,))
@@ -294,6 +308,7 @@
             pltpu.SemaphoreType.DMA((10,)),
             pltpu.SemaphoreType.DMA((10,)),
             pltpu.SemaphoreType.DMA((frames // 2,)),
+            pltpu.SemaphoreType.REGULAR,
         ],
         compiler_params=pltpu.CompilerParams(
             collective_id=0, has_side_effects=True, vmem_limit_bytes=56 * 2**20

time: 25.6 us -> 26.4 us (1.031)
  the two profiles are of different devices: /device:TPU:2 before, /device:TPU:121 now
where the time goes in v7:
time: 26.4 us; the launch traced here: 26.3 us
  Pallas kernels  24.3 us (92%)
  local copies, waits for them, and re-layouts  1.94 us (7%)
    pallas_call x1, Pallas kernels, per_device(): pl.pallas_call(kernel, out_shape=jax.ShapeDtypeStruct((frames // 2, rows,...  24.3 us
    unnamed x1, local copies, waits for them, and re-layouts  1.94 us

profile of v7, /device:TPU:121, one launch (start us, length us, event | category | flops | bytes accessed | tf_op | source)
XLA Modules:
  0.0 26.3 jit_solution(15772303581189550367)
XLA Ops:
  0.0 24.3 %residual_block.1 = bf16[3,8,32,384]{3,2,1,0:T(8,128)(2,1)} custom-call(bf16[6,8,32,384]{3,2,1,0:T(8,128)(2,1)} %x_ref.1, f32[384]{0:T(512)} %gain_ref.1, bf16[3,3456,384]{2,1,0:T(8,128)(2,1)} %bitcast.2, f32[384]{0:T(512)} %cb_ref.1, bf16[1152,384]{1,0:T(8,128)(2,1)} %bitcast.3, f32[384]{0:T(512)} %tb_ref.1, s32[16]{0:T(128)} %clips_ref.1), custom_call_target="tpu_custom_call" | custom-call | flops 12910067712 | bytes 12000000 | tf_op jit(solution)/shard_map/residual_block/pallas_call | solution.py:287
  24.3 1.9 %copy.9 = bf16[3,8,32,384]{3,2,1,0:T(8,128)(2,1)} copy(bf16[3,8,32,384]{3,2,1,0:T(8,128)(2,1)} %residual_block.1) | data formatting | bytes 1179648

commit v8 on v5

--- a/solution.py
+++ b/solution.py
@@ -9,7 +9,6 @@
 BF16 = jnp.bfloat16
 MESH = pl.DeviceIdType.MESH
 TAPS = 3
-PIECE = 256
 
 
 def kernel(
@@ -110,12 +109,9 @@
         )
         taps = [k for k in range(TAPS) if 0 <= sources[0] - k < frames]
         deepest, stop = slice(first * deep, (first + count) * deep), (taps[-1] + 1) * width
-        pieces = []
-        for column in range(taps[0] * width, stop, PIECE):
-            columns = slice(column, min(column + PIECE, stop))
-            pieces.append(jnp.dot(left, weight[deepest, columns], preferred_element_type=F32))
-            beside(rate)
-        product = jnp.concatenate(pieces, 1)
+        columns = slice(taps[0] * width, stop)
+        product = jnp.dot(left, weight[deepest, columns], preferred_element_type=F32)
+        beside(rate)
         size = left.shape[0] // len(sources)
         sums = {}
         for i, s in enumerate(sources):
@@ -162,8 +158,7 @@
         queue.extend((lag + t, r) for r in range(1, rows + 1))
     for copy in head:
         copy.wait()
-    for s in (5, 4, 3):
-        conv((s,), inner, 0, 1, rate=1)
+    conv((5,), inner, 0, 1, rate=5)
 
     def count(condition):
         return jnp.where(condition, 1, 0)
@@ -222,18 +217,21 @@
         ),
     ]
 
+    for s in (4, 3):
+        conv((s,), inner, 0, 1, rate=5)
     for copy in tail + small[1:]:
         copy.wait()
-    for s in (5, 4, 3):
-        conv((s,), inner, 1, 2, rate=1)
-    for copy in middle + outer:
+    for s in (5, 4):
+        conv((s,), inner, 1, 2, rate=5)
+    for copy in middle:
         copy.wait_recv()
-    for s in (5, 4, 3):
-        normalize(s, 0)
-        normalize(s, rows + 1)
+    queue[:0] = [(s, r) for s in (5, 4, 3) for r in (0, rows + 1)]
+    conv((3,), inner, 1, 2, rate=10)
+    for copy in outer:
+        copy.wait_recv()
     queue[:0] = [(s, r) for s in (7, 6) for r in (0, rows + 1)]
     queue.extend((2, r) for r in (0, rows + 1))
-    conv((5, 4, 3), edge, rate=2)
+    conv((5, 4, 3), edge, rate=10)
     finish(3, total[3])
     beside(len([item for item in queue if item[0] > 2]))
     conv((7,), whole)
@@ -241,8 +239,6 @@
     before_copy = Send(5, resid.at[frames], before, (seq + 1, sp), has_next, has_back)
     time_load.wait()
     outs = [project(2)]
-    for copy in earlier:
-        copy.wait_recv()
     opening = jnp.int32(0)
     start = jnp.int32(0)
     for j in range(clips.shape[0]):
@@ -250,8 +246,12 @@
         start = start + clips[j]
     keep = (1 - opening).astype(F32)
     beside(len(queue))
-    queue.extend((s, r, keep) for s in reversed(range(lag)) for r in range(rows + 2))
-    conv((2,), whole, final=(2,), rate=4)
+    conv((2,), whole, final=(2,))
+    for copy in earlier:
+        copy.wait_recv()
+    for s in reversed(range(lag)):
+        for r in range(rows + 2):
+            normalize(s, r, keep)
     conv((1,), whole, final=(1,))
     outs.append(project(1))
     conv((0,), whole, final=(0,))

time: 25.6 us -> 24.6 us (0.961)
  the two profiles are of different devices: /device:TPU:2 before, /device:TPU:121 now
where the time goes in v8:
time: 24.6 us; the launch traced here: 24.5 us
  Pallas kernels  22.6 us (92%)
  local copies, waits for them, and re-layouts  1.94 us (8%)
    pallas_call x1, Pallas kernels, per_device(): pl.pallas_call(kernel, out_shape=jax.ShapeDtypeStruct((frames // 2, rows,...  22.6 us
    unnamed x1, local copies, waits for them, and re-layouts  1.94 us

profile of v8, /device:TPU:121, one launch (start us, length us, event | category | flops | bytes accessed | tf_op | source)
XLA Modules:
  0.0 24.5 jit_solution(11858652368979886232)
XLA Ops:
  0.0 22.6 %residual_block.1 = bf16[3,8,32,384]{3,2,1,0:T(8,128)(2,1)} custom-call(bf16[6,8,32,384]{3,2,1,0:T(8,128)(2,1)} %x_ref.1, f32[384]{0:T(512)} %gain_ref.1, bf16[3,3456,384]{2,1,0:T(8,128)(2,1)} %bitcast.2, f32[384]{0:T(512)} %cb_ref.1, bf16[1152,384]{1,0:T(8,128)(2,1)} %bitcast.3, f32[384]{0:T(512)} %tb_ref.1, s32[16]{0:T(128)} %clips_ref.1), custom_call_target="tpu_custom_call" | custom-call | flops 12910067712 | bytes 12000000 | tf_op jit(solution)/shard_map/residual_block/pallas_call | solution.py:273
  22.6 1.9 %copy.9 = bf16[3,8,32,384]{3,2,1,0:T(8,128)(2,1)} copy(bf16[3,8,32,384]{3,2,1,0:T(8,128)(2,1)} %residual_block.1) | data formatting | bytes 1179648
